TPU v7x, 32 devices: a whole 2x2x4 slice. The times are simulated.
32 devices in a mesh: prod: 4 (over y, x), cand: 8 (over z, core).
Axes of the slice: x: 2, y: 2, z: 4, core: 2. Of those that a mesh axis runs over, the one named last changes fastest.
Arguments:
- cand_states: bfloat16 [4, 8, 128, 4096], P('prod', 'cand'), may hold values from -600 to 600
- enc_rows: bfloat16 [4, 256, 4096], P('prod', 'cand'), may hold values from -120 to 120
- w_query: bfloat16 [4096, 4096], P('prod', 'cand'), may hold values from -0.09375 to 0.09375
- w_key: bfloat16 [4096, 4096], P('prod', 'cand'), may hold values from -0.09375 to 0.09375
- w_value: bfloat16 [4096, 4096], P('prod', 'cand'), may hold values from -0.09375 to 0.09375
- w_out: bfloat16 [4096, 4096], P('cand', 'prod'), may hold values from -0.375 to 0.375
- tile_mask: int32 [4, 8, 2], P('prod', 'cand'), may hold values from 0 to 1, as said below
- counts: int32 [4], P('prod'), may hold values from 1 to 8, as said below
Outputs:
- cross_out: bfloat16 [4, 8, 128, 4096], P('prod', 'cand')
Inputs may be any that keep to these rules, and one draw needn't show every extreme that they name: `tile_mask`: every candidate has at least one tile set. `counts`: some product fills all 8 slots.
All inputs are finite; a program needn't handle non-finite values.
Results may differ from a plain program's by a relative error of at most 0.023.
The roundings to bfloat16 on the way count: a program that leaves them out, or rounds other values in their place, can miss the bound.
Values may be sent and summed in bfloat16 or wider, within the bound.
No kernel may reach another device: no remote copies, remote signals or barrier semaphores. Data moves between devices by JAX's collectives and lax.ppermute only.
A program may use at most 128 MiB of HBM per device.

v0:
```python
import functools

import jax
import jax.numpy as jnp
from jax import lax
from jax.experimental import pallas as pl
from jax.experimental.pallas import tpu as pltpu
from jax.sharding import PartitionSpec as P

HD = 64
TILE = 128
LANES = 128
FLAG_ROWS = 16
VMEM = pltpu.CompilerParams(vmem_limit_bytes=40 * 1024 * 1024)


def ring_order(chips):
    odd = list(range(1, chips, 2))
    even = list(range(2, chips, 2))
    return [0] + odd + even[::-1]


def small(flops=1):
    return pl.CostEstimate(flops=flops, bytes_accessed=1, transcendentals=0)


def columns_kernel(ids, x_ref, *outs):
    block = outs[0].shape[1]
    for r, out in enumerate(outs):
        source = jnp.bitwise_xor(ids[0], r)
        out[...] = x_ref[:, pl.ds(pl.multiple_of(source * block, block), block)]


def column_blocks(ids, x, parts):
    shape = jax.ShapeDtypeStruct((x.shape[0], x.shape[1] // parts), x.dtype)
    return pl.pallas_call(
        columns_kernel,
        out_shape=[shape] * parts,
        in_specs=[
            pl.BlockSpec(memory_space=pltpu.SMEM),
            pl.BlockSpec(memory_space=pltpu.VMEM),
        ],
        out_specs=[pl.BlockSpec(memory_space=pltpu.VMEM)] * parts,
        compiler_params=VMEM,
        cost_estimate=small(),
        name="columns",
    )(ids, x)


def key_value_kernel(parts, rows, tiles, enc_ref, w_key, w_value, open_ref, *outs):
    slots, height, block = enc_ref.shape
    local = w_key.shape[1]
    elen = slots * rows
    encoder = jnp.concatenate([enc_ref[slot, : parts * rows, :] for slot in range(slots)], axis=0)
    for column, weight in ((0, w_key), (local, w_value)):
        sums = jnp.dot(encoder, weight[...], preferred_element_type=jnp.float32)
        for r, out in enumerate(outs):
            for slot in range(slots):
                start, target = (slot * parts + r) * rows, slot * rows
                out[target : target + rows, column : column + local] = sums[
                    start : start + rows
                ].astype(out.dtype)
    tile = lax.broadcasted_iota(jnp.int32, (1, elen), 1) // TILE
    for slot in range(slots):
        seen = jnp.zeros((1, elen), jnp.float32)
        for t in range(tiles):
            start = t * (block // tiles)
            flag = enc_ref[slot, height - 1 : height, start : start + elen].astype(jnp.float32)
            seen = jnp.where(tile == t, flag, seen)
        open_ref[slot : slot + 1, :] = seen


def key_value(gathered, w_key, w_value, parts, rows, tiles):
    slots, local = gathered.shape[0], w_key.shape[1]
    elen = slots * rows
    return pl.pallas_call(
        functools.partial(key_value_kernel, parts, rows, tiles),
        out_shape=[jax.ShapeDtypeStruct((slots, elen), jnp.float32)]
        + [
            jax.ShapeDtypeStruct((elen, 2 * local), jnp.bfloat16 if r else jnp.float32)
            for r in range(parts)
        ],
        in_specs=[pl.BlockSpec(memory_space=pltpu.VMEM)] * 3,
        out_specs=[pl.BlockSpec(memory_space=pltpu.VMEM)] * (parts + 1),
        compiler_params=pltpu.CompilerParams(vmem_limit_bytes=58 * 1024 * 1024),
        cost_estimate=small(3 * 10**9),
        name="key_value",
    )(gathered, w_key, w_value)


def query_kernel(pieces, parts, ids, mine, sib, *refs):
    weights, out_ref = refs[:pieces], refs[pieces]
    clen, width = mine.shape
    block = width // parts
    scales = []
    for ref in (mine, sib):
        values = ref[...].astype(jnp.float32)
        scales.append(lax.rsqrt(jnp.sum(values * values, axis=-1, keepdims=True) / width + 1e-06))
    total, start = None, 0
    for weight in weights:
        depth = weight.shape[0]
        from_prod = jnp.bitwise_xor(ids[0], start // block)
        source = pl.multiple_of(from_prod * block + start % block, LANES)
        rows = jnp.concatenate(
            [
                (ref[:, pl.ds(source, depth)].astype(jnp.float32) * scale).astype(jnp.bfloat16)
                for ref, scale in zip((mine, sib), scales)
            ],
            axis=0,
        )
        term = jnp.dot(rows, weight[...], preferred_element_type=jnp.float32)
        total = term if total is None else total + term
        start += depth
    out_ref[...] = total.astype(jnp.bfloat16)


def query(ids, mine, sib, weights, parts):
    clen = mine.shape[0]
    return pl.pallas_call(
        functools.partial(query_kernel, len(weights), parts),
        out_shape=jax.ShapeDtypeStruct((2 * clen, weights[0].shape[1]), jnp.bfloat16),
        in_specs=[pl.BlockSpec(memory_space=pltpu.SMEM)]
        + [pl.BlockSpec(memory_space=pltpu.VMEM)] * (2 + len(weights)),
        out_specs=pl.BlockSpec(memory_space=pltpu.VMEM),
        compiler_params=VMEM,
        cost_estimate=small(),
        name="query",
    )(ids, mine, sib, *weights)


def attend_kernel(order, step, ids, query_ref, open_ref, kv_ref, out_ref):
    chips = len(order)
    chip, core = lax.div(ids[1], 2), lax.rem(ids[1], 2)
    source = chip
    if step:
        for place in range(chips):
            source = jnp.where(chip == order[place], order[(place - step) % chips], source)
    who = (2 * source + core, 2 * source + 1 - core)
    clen = query_ref.shape[0] // 2
    elen, local = kv_ref.shape[0], kv_ref.shape[1] // 2
    is_open = (
        jnp.concatenate(
            [jnp.broadcast_to(open_ref[pl.ds(who[i], 1), :], (clen, elen)) for i in range(2)],
            axis=0,
        )
        > 0.5
    )
    lane = lax.broadcasted_iota(jnp.int32, (elen, LANES), 1) // HD
    for pair in range(local // LANES):
        columns = slice(pair * LANES, (pair + 1) * LANES)
        keys = kv_ref[:, columns]
        values = kv_ref[:, local + pair * LANES : local + (pair + 1) * LANES]
        context = None
        for half in range(LANES // HD):
            own = lane == half
            scores = (
                lax.dot_general(
                    query_ref[:, columns],
                    jnp.where(own, keys, jnp.zeros_like(keys)),
                    (((1,), (1,)), ((), ())),
                    preferred_element_type=jnp.float32,
                )
                * 0.125
            )
            scores = jnp.where(is_open, scores, -1e30)
            top = jnp.max(scores, axis=-1, keepdims=True)
            grown = jnp.exp(scores - top)
            probs = (grown / jnp.sum(grown, axis=-1, keepdims=True)).astype(jnp.bfloat16)
            term = jnp.dot(
                probs,
                jnp.where(own, values, jnp.zeros_like(values)),
                preferred_element_type=jnp.float32,
            )
            context = term if context is None else context + term
        out_ref[:, columns] = context.astype(jnp.bfloat16)


def attend(order, step, ids, queries, is_open, kv):
    return pl.pallas_call(
        functools.partial(attend_kernel, order, step),
        out_shape=jax.ShapeDtypeStruct(queries.shape, jnp.bfloat16),
        in_specs=[pl.BlockSpec(memory_space=pltpu.SMEM)]
        + [pl.BlockSpec(memory_space=pltpu.VMEM)] * 3,
        out_specs=pl.BlockSpec(memory_space=pltpu.VMEM),
        compiler_params=VMEM,
        cost_estimate=small(),
        name="attend",
    )(ids, queries, is_open, kv)


def project_kernel(pieces, context_ref, *refs):
    weights, (mine, sib) = refs[: len(pieces)], refs[len(pieces) :]
    clen = mine.shape[0]
    totals = {}
    for (r, row), weight in zip(pieces, weights):
        term = jnp.dot(
            context_ref[:, row : row + weight.shape[0]],
            weight[...],
            preferred_element_type=jnp.float32,
        )
        totals[r] = term if r not in totals else totals[r] + term
        if row + weight.shape[0] == context_ref.shape[1]:
            block = weight.shape[1]
            rows = totals[r].astype(jnp.bfloat16)
            mine[:, r * block : (r + 1) * block] = rows[:clen]
            sib[:, r * block : (r + 1) * block] = rows[clen:]


def project(context, weights):
    rows, local = context.shape
    pieces, row = [], 0
    for weight in weights:
        pieces.append((row // local, row % local))
        row += weight.shape[0]
    width = row // local * weights[0].shape[1]
    shape = jax.ShapeDtypeStruct((rows // 2, width), jnp.bfloat16)
    return pl.pallas_call(
        functools.partial(project_kernel, pieces),
        out_shape=[shape, shape],
        in_specs=[pl.BlockSpec(memory_space=pltpu.VMEM)] * (1 + len(weights)),
        out_specs=[pl.BlockSpec(memory_space=pltpu.VMEM)] * 2,
        compiler_params=VMEM,
        cost_estimate=small(),
        name="project",
    )(context, *weights)


def finish_kernel(parts, ids, counts, *refs):
    out_ref = refs[-1]
    chunks = (len(refs) - 1) // 3
    block = out_ref.shape[1] // parts
    live = jnp.where(ids[1] < counts[0], 1.0, 0.0)
    r = 0
    for chunk in range(chunks):
        mine, other, passed = refs[3 * chunk : 3 * chunk + 3]
        for start in range(0, mine.shape[1], block):
            columns = slice(start, start + block)
            total = mine[:, columns].astype(jnp.float32) + other[:, columns].astype(jnp.float32)
            total = total + passed[:, columns].astype(jnp.float32)
            target = pl.multiple_of(jnp.bitwise_xor(ids[0], r) * block, block)
            out_ref[:, pl.ds(target, block)] = (total * live).astype(jnp.bfloat16)
            r += 1


def finish(ids, counts, sums, parts, width):
    return pl.pallas_call(
        functools.partial(finish_kernel, parts),
        out_shape=jax.ShapeDtypeStruct((sums[0].shape[0], width), jnp.bfloat16),
        in_specs=[pl.BlockSpec(memory_space=pltpu.SMEM)] * 2
        + [pl.BlockSpec(memory_space=pltpu.VMEM)] * len(sums),
        out_specs=pl.BlockSpec(memory_space=pltpu.VMEM),
        compiler_params=VMEM,
        cost_estimate=small(),
        name="finish",
    )(ids, counts, *sums)


def shards(parts, devices, cand_states, enc_rows, w_query, w_key, w_value, w_out, tile_mask, counts):
    chips = devices // 2
    order = ring_order(chips)
    along = [
        (2 * order[i] + core, 2 * order[(i + 1) % chips] + core)
        for i in range(chips)
        for core in range(2)
    ]
    across = [(c, c ^ 1) for c in range(devices)]

    def to_next(value):
        return lax.ppermute(value, "cand", along)

    def to_sib(value):
        return lax.ppermute(value, "cand", across)

    def flip(value, r):
        return lax.ppermute(value, "prod", [(q, q ^ r) for q in range(parts)])

    ids = jnp.stack([lax.axis_index("prod"), lax.axis_index("cand")]).astype(jnp.int32)

    barrier = lax.optimization_barrier
    f32, bf16 = jnp.float32, jnp.bfloat16

    def near_blocks(weight):
        return [flip(weight, r) for r in range(1, min(parts, 3))]

    def far_blocks(weight, near):
        if parts != 4:
            return [flip(weight, r) for r in range(3, parts)]
        half = weight.shape[0] // 2
        return [flip(near[0][:half], 2), flip(near[1][half:], 1)]

    clen, width = cand_states.shape[2:]
    states = cand_states.reshape(clen, width)
    pairs = [(states, to_sib(states))]
    cut = clen // 4
    top = to_next(states[:cut])

    rows = enc_rows.shape[1]
    block = width // parts
    columns = column_blocks(ids, enc_rows.reshape(rows, width), parts)
    columns = [columns[0]] + [flip(columns[r], r) for r in range(1, parts)]
    columns, w_query = barrier((columns, w_query))
    tiles = tile_mask.shape[2]
    flags = tile_mask.reshape(1, tiles, 1).astype(bf16)
    flags = jnp.broadcast_to(flags, (FLAG_ROWS, tiles, block // tiles)).reshape(FLAG_ROWS, block)
    piece = jnp.concatenate(columns + [flags], axis=0)
    piece, top = barrier((piece, top))
    gathered = lax.all_gather(piece, "cand", axis=0)
    states = jnp.concatenate([top, to_next(states[cut:])], axis=0)
    pairs.append((states, to_sib(states)))
    for hop in range(2, chips):
        states = to_next(states)
        pairs.append((states, to_sib(states)))

    near = near_blocks(w_query)
    query_parts = [w_query] + near + far_blocks(w_query, near)
    near, w_out = barrier((near, w_out))
    out_near = near_blocks(w_out)

    is_open, *sums = key_value(gathered, w_key, w_value, parts, rows, tiles)
    sums, out_near = barrier((sums, out_near))
    out_parts = [w_out] + out_near + far_blocks(w_out, out_near)
    out_chunks = [out_parts[: parts // 2], out_parts[parts // 2 :]]
    kv = sums[0]
    for r in range(1, parts):
        kv = kv + flip(sums[r], r).astype(f32)
    kv = kv.astype(bf16)

    steps = list(range(1, chips)) + [0]
    passed = [None] * len(out_chunks)
    queries = [query(ids, *pairs[step], query_parts, parts) for step in steps]
    for index, step in enumerate(steps):
        context = attend(order, step, ids, queries[index], is_open, kv)
        last, totals = [], []
        for chunk, weights in enumerate(out_chunks):
            if index == 1 and not chunk:
                context, passed[0] = barrier((context, passed[0]))
            mine, sib = project(context, weights)
            other = to_sib(sib)
            last += [mine, other, passed[chunk]]
            total = mine.astype(f32) + other.astype(f32)
            if index:
                total = total + passed[chunk].astype(f32)
            totals.append(total.astype(bf16))
        if not index:
            totals[1], queries[1] = barrier((totals[1], queries[1]))
        if step:
            passed = [to_next(total) for total in totals]
    return finish(ids, counts, last, parts, width).reshape(cand_states.shape)


def solution(mesh):
    parts, devices = mesh.shape["prod"], mesh.shape["cand"]
    return jax.shard_map(
        functools.partial(shards, parts, devices),
        mesh=mesh,
        in_specs=(
            P("prod", "cand", None, None),
            P("prod", "cand", None),
            P("prod", "cand"),
            P("prod", "cand"),
            P("prod", "cand"),
            P("cand", "prod"),
            P("prod", "cand", None),
            P("prod"),
        ),
        out_specs=P("prod", "cand", None, None),
        check_vma=False,
    )
```

profile of v0, /device:TPU:0, one launch (start us, length us, event | category | flops | bytes accessed | tf_op | source)
XLA Modules:
  0.0 205.6 jit_solution(13746933472207387594)
XLA Ops:
  6.6 0.9 copy-done.4
  7.6 0.6 columns.1
  8.1 3.0 %collective-permute-start.1 = (bf16[32,1024]{1,0:T(8,128)(2,1)S(1)}, bf16[32,1024]{1,0:T(8,128)(2,1)S(1)}, u32[]{:S(2)}, u32[]{:S(2)}) collective-permute-start(bf16[32,1024]{1,0:T(8,128)(2,1)S(1)} %get-tuple-element.49), channel_id=1, source_target_pairs={{0,8},{8,0},{16,24},{24,16},{1,9},{9,1},{17,25},{25,17},{2,10},{10... | collective-permute-start | bytes 196616 | tf_op jit(solution)/shard_map/ppermute | solution.py:275
  11.1 1.5 collective-permute-start.2
  12.7 1.0 slice_bitcast_fusion.1
  13.6 2.1 %collective-permute-start.8 = (bf16[32,4096]{1,0:T(8,128)(2,1)S(1)}, bf16[32,4096]{1,0:T(8,128)(2,1)S(1)}, u32[]{:S(2)}, u32[]{:S(2)}) collective-permute-start(bf16[32,4096]{1,0:T(8,128)(2,1)S(1)} %slice_bitcast_fusion.1), channel_id=1, source_target_pairs={{0,2},{1,3},{2,6},{3,7},{6,4},{7,5},{4,0},{5,1},{8,10},{9,11},{10,... | collective-permute-start | bytes 786440 | tf_op jit(solution)/shard_map/ppermute | solution.py:269
  15.7 0.7 convert_bitcast_fusion
  16.5 1.3 collective-permute-done.3
  17.9 4.3 %collective-permute-done.8 = bf16[32,4096]{1,0:T(8,128)(2,1)S(1)} collective-permute-done((bf16[32,4096]{1,0:T(8,128)(2,1)S(1)}, bf16[32,4096]{1,0:T(8,128)(2,1)S(1)}, u32[]{:S(2)}, u32[]{:S(2)}) %collective-permute-start.8) | collective-permute-done | bytes 262176 | tf_op jit(solution)/shard_map/ppermute | solution.py:269
  22.2 1.6 collective-permute-start.4
  23.8 1.5 collective-permute-start.5
  25.4 1.2 slice_bitcast_fusion
  26.6 0.8 collective-permute-start.15
  27.4 18.5 %collective-permute-done.4.refs_1_ = bf16[1024,512]{1,0:T(8,128)(2,1)S(1)} collective-permute-done((bf16[1024,512]{1,0:T(8,128)(2,1)}, bf16[1024,512]{1,0:T(8,128)(2,1)S(1)}, u32[]{:S(2)}, u32[]{:S(2)}) %collective-permute-start.4) | collective-permute-done | bytes 1048608 | tf_op jit(solution)/shard_map/ppermute | solution.py:275
  45.9 1.1 collective-permute-done.5.refs_2_
  47.1 1.5 collective-permute-start.10
  48.6 0.7 constant_dynamic-update-slice_fusion.6
  49.3 0.5 collective-permute-start.9
  49.8 15.6 %collective-permute-done.15 = bf16[96,4096]{1,0:T(8,128)(2,1)S(1)} collective-permute-done((bf16[96,4096]{1,0:T(8,128)(2,1)S(1)}, bf16[96,4096]{1,0:T(8,128)(2,1)S(1)}, u32[]{:S(2)}, u32[]{:S(2)}) %collective-permute-start.15) | collective-permute-done | bytes 786464 | tf_op jit(solution)/shard_map/ppermute | solution.py:269
  65.4 1.0 constant_dynamic-update-slice_fusion.5.mine
  66.8 0.9 slice.32
  67.7 1.5 collective-permute-start.6
  69.2 0.9 slice.33
  70.4 6.3 %key_value.1 = (f32[8,256]{1,0:T(8,128)}, f32[256,1024]{1,0:T(8,128)}, bf16[256,1024]{1,0:T(8,128)(2,1)}, bf16[256,1024]{1,0:T(8,128)(2,1)}, bf16[256,1024]{1,0:T(8,128)(2,1)}) custom-call(bf16[8,144,1024]{2,1,0:T(8,128)(2,1)} %bitcast.19, bf16[1024,512]{1,0:T(8,128)(2,1)} %w_key.1, bf16[1024,512]{1,0:T(8,128)(2,1)} %w_value.1), custom_call_target="tpu_custom_call" | custom-call | flops 3000000000 | bytes 1 | tf_op jit(solution)/shard_map/key_value/pallas_call | solution.py:76
  76.7 1.7 collective-permute-start.11
  78.4 3.9 %collective-permute-done.6.refs_3_ = bf16[512,512]{1,0:T(8,128)(2,1)} collective-permute-done((bf16[512,512]{1,0:T(8,128)(2,1)}, bf16[512,512]{1,0:T(8,128)(2,1)}, u32[]{:S(2)}, u32[]{:S(2)}) %collective-permute-start.6) | collective-permute-done | bytes 524320 | tf_op jit(solution)/shard_map/ppermute | solution.py:275
  82.3 1.5 collective-permute-start.12
  83.8 1.3 collective-permute-done.7.refs_4_
  85.1 1.5 collective-permute-start.13
  86.6 3.4 %collective-permute-start.17 = (bf16[128,4096]{1,0:T(8,128)(2,1)}, bf16[128,4096]{1,0:T(8,128)(2,1)S(1)}, u32[]{:S(2)}, u32[]{:S(2)}) collective-permute-start(bf16[128,4096]{1,0:T(8,128)(2,1)} %collective-permute-done.16.mine), channel_id=1, source_target_pairs={{0,2},{1,3},{2,6},{3,7},{6,4},{7,5},{4,0},{5,1},{8,10},{9,11},{10,... | collective-permute-start | bytes 3145736 | tf_op jit(solution)/shard_map/ppermute | solution.py:269
  90.0 3.5 %query.6.query_ref = bf16[256,512]{1,0:T(8,128)(2,1)S(1)} custom-call(s32[2]{0:T(128)S(1)} %pad_add_fusion.ids, bf16[128,4096]{1,0:T(8,128)(2,1)} %constant_dynamic-update-slice_fusion.5.mine, bf16[128,4096]{1,0:T(8,128)(2,1)} %collective-permute-done.20.sib, bf16[1024,512]{1,0:T(8,128)(2,1)S(1)} %copy-done.2, ...), custom_call_target="tpu_custom_call" | custom-call | flops 1 | bytes 1 | tf_op jit(solution)/shard_map/query/pallas_call | solution.py:119
  93.7 2.6 %collective-permute-done.11 = bf16[256,1024]{1,0:T(8,128)(2,1)S(1)} collective-permute-done((bf16[256,1024]{1,0:T(8,128)(2,1)}, bf16[256,1024]{1,0:T(8,128)(2,1)S(1)}, u32[]{:S(2)}, u32[]{:S(2)}) %collective-permute-start.11) | collective-permute-done | bytes 524320 | tf_op jit(solution)/shard_map/ppermute | solution.py:275
  96.3 0.9 collective-permute-start.21
  97.2 10.4 %collective-permute-done.12 = bf16[256,1024]{1,0:T(8,128)(2,1)S(1)} collective-permute-done((bf16[256,1024]{1,0:T(8,128)(2,1)}, bf16[256,1024]{1,0:T(8,128)(2,1)S(1)}, u32[]{:S(2)}, u32[]{:S(2)}) %collective-permute-start.12) | collective-permute-done | bytes 524320 | tf_op jit(solution)/shard_map/ppermute | solution.py:275
  107.5 1.7 collective-permute-start.22
  109.6 2.3 %attend.6.context_ref = bf16[256,512]{1,0:T(8,128)(2,1)S(1)} custom-call(s32[2]{0:T(128)S(1)} %pad_add_fusion.ids, bf16[256,512]{1,0:T(8,128)(2,1)S(1)} %query.6.query_ref, f32[8,256]{1,0:T(8,128)S(1)} %copy-done.5, bf16[256,1024]{1,0:T(8,128)(2,1)S(1)} %add_convert_fusion.6.kv_ref), custom_call_target="tpu_custom_call" | custom-call | flops 1 | bytes 1 | tf_op jit(solution)/shard_map/attend/pallas_call | solution.py:179
  111.8 1.9 project.11
  113.9 4.7 %collective-permute-done.21.refs_1_ = bf16[256,1024]{1,0:T(8,128)(2,1)S(1)} collective-permute-done((bf16[256,1024]{1,0:T(8,128)(2,1)S(1)}, bf16[256,1024]{1,0:T(8,128)(2,1)S(1)}, u32[]{:S(2)}, u32[]{:S(2)}) %collective-permute-start.21) | collective-permute-done | bytes 524320 | tf_op jit(solution)/shard_map/ppermute | solution.py:275
  118.5 0.7 project.10
  119.4 0.5 collective-permute-start.18
  120.0 3.5 %collective-permute-start.26 = (bf16[128,2048]{1,0:T(8,128)(2,1)S(1)}, bf16[128,2048]{1,0:T(8,128)(2,1)S(1)}, u32[]{:S(2)}, u32[]{:S(2)}) collective-permute-start(bf16[128,2048]{1,0:T(8,128)(2,1)S(1)} %add_convert_fusion.4), channel_id=1, source_target_pairs={{0,2},{1,3},{2,6},{3,7},{6,4},{7,5},{4,0},{5,1},{8,10},{9,11},{10,... | collective-permute-start | bytes 1572872 | tf_op jit(solution)/shard_map/ppermute | solution.py:269
  123.5 3.2 %query.7.query_ref = bf16[256,512]{1,0:T(8,128)(2,1)S(1)} custom-call(s32[2]{0:T(128)S(1)} %pad_add_fusion.ids, bf16[128,4096]{1,0:T(8,128)(2,1)} %collective-permute-done.16.mine, bf16[128,4096]{1,0:T(8,128)(2,1)S(1)} %collective-permute-done.24.sib, bf16[1024,512]{1,0:T(8,128)(2,1)S(1)} %copy-done.2, bf16[1024,512]{1,0:T(8,128)(2,1)S(1)} %collective-permute-done.4.refs_1_, ...), custom_call_target="tpu_custom_call" | custom-call | flops 1 | bytes 1 | tf_op jit(solution)/shard_map/query/pallas_call | solution.py:119
  126.9 2.3 %attend.7.context_ref = bf16[256,512]{1,0:T(8,128)(2,1)S(1)} custom-call(s32[2]{0:T(128)S(1)} %pad_add_fusion.ids, bf16[256,512]{1,0:T(8,128)(2,1)S(1)} %query.7.query_ref, f32[8,256]{1,0:T(8,128)S(1)} %copy-done.5, bf16[256,1024]{1,0:T(8,128)(2,1)S(1)} %add_convert_fusion.6.kv_ref), custom_call_target="tpu_custom_call" | custom-call | flops 1 | bytes 1 | tf_op jit(solution)/shard_map/attend/pallas_call | solution.py:179
  129.4 6.4 %collective-permute-done.26 = bf16[128,2048]{1,0:T(8,128)(2,1)S(1)} collective-permute-done((bf16[128,2048]{1,0:T(8,128)(2,1)S(1)}, bf16[128,2048]{1,0:T(8,128)(2,1)S(1)}, u32[]{:S(2)}, u32[]{:S(2)}) %collective-permute-start.26) | collective-permute-done | bytes 524320 | tf_op jit(solution)/shard_map/ppermute | solution.py:269
  135.8 0.7 project.15
  137.1 1.9 project.12
  139.2 2.9 %query.5.query_ref = bf16[256,512]{1,0:T(8,128)(2,1)S(1)} custom-call(s32[2]{0:T(128)S(1)} %pad_add_fusion.ids, bf16[128,4096]{1,0:T(8,128)(2,1)S(1)} %collective-permute-done.17.mine, bf16[128,4096]{1,0:T(8,128)(2,1)S(1)} %collective-permute-done.18.sib, bf16[1024,512]{1,0:T(8,128)(2,1)S(1)} %copy-done.2, ...), custom_call_target="tpu_custom_call" | custom-call | flops 1 | bytes 1 | tf_op jit(solution)/shard_map/query/pallas_call | solution.py:119
  142.1 2.3 %attend.5.context_ref = bf16[256,512]{1,0:T(8,128)(2,1)S(1)} custom-call(s32[2]{0:T(128)S(1)} %pad_add_fusion.ids, bf16[256,512]{1,0:T(8,128)(2,1)S(1)} %query.5.query_ref, f32[8,256]{1,0:T(8,128)S(1)} %copy-done.5, bf16[256,1024]{1,0:T(8,128)(2,1)S(1)} %add_convert_fusion.6.kv_ref), custom_call_target="tpu_custom_call" | custom-call | flops 1 | bytes 1 | tf_op jit(solution)/shard_map/attend/pallas_call | solution.py:179
  144.3 1.9 project.9
  146.3 0.7 project.14
  147.0 0.5 collective-permute-start.31
  147.8 2.5 %collective-permute-start.34 = (bf16[128,2048]{1,0:T(8,128)(2,1)S(1)}, bf16[128,2048]{1,0:T(8,128)(2,1)S(1)}, u32[]{:S(2)}, u32[]{:S(2)}) collective-permute-start(bf16[128,2048]{1,0:T(8,128)(2,1)S(1)} %add_convert_fusion.1), channel_id=1, source_target_pairs={{0,2},{1,3},{2,6},{3,7},{6,4},{7,5},{4,0},{5,1},{8,10},{9,11},{10,... | collective-permute-start | bytes 1572872 | tf_op jit(solution)/shard_map/ppermute | solution.py:269
  150.6 0.9 collective-permute-start.28
  151.5 2.9 %query.4.query_ref = bf16[256,512]{1,0:T(8,128)(2,1)S(1)} custom-call(s32[2]{0:T(128)S(1)} %pad_add_fusion.ids, bf16[128,4096]{1,0:T(8,128)(2,1)S(1)} %bitcast.16, bf16[128,4096]{1,0:T(8,128)(2,1)S(1)} %collective-permute-done.sib, bf16[1024,512]{1,0:T(8,128)(2,1)S(1)} %copy-done.2, bf16[1024,512]{1,0:T(8,128)(2,1)S(1)} %collective-permute-done.4.refs_1_, ...), custom_call_target="tpu_custom_call" | custom-call | flops 1 | bytes 1 | tf_op jit(solution)/shard_map/query/pallas_call | solution.py:119
  154.5 2.2 %attend.4.context_ref = bf16[256,512]{1,0:T(8,128)(2,1)S(1)} custom-call(s32[2]{0:T(128)S(1)} %pad_add_fusion.ids, bf16[256,512]{1,0:T(8,128)(2,1)S(1)} %query.4.query_ref, f32[8,256]{1,0:T(8,128)S(1)} %copy-done.5, bf16[256,1024]{1,0:T(8,128)(2,1)S(1)} %add_convert_fusion.6.kv_ref), custom_call_target="tpu_custom_call" | custom-call | flops 1 | bytes 1 | tf_op jit(solution)/shard_map/attend/pallas_call | solution.py:179
  156.7 1.9 project.8
  158.7 0.7 project.13
  160.0 3.6 %collective-permute-done.34 = bf16[128,2048]{1,0:T(8,128)(2,1)S(1)} collective-permute-done((bf16[128,2048]{1,0:T(8,128)(2,1)S(1)}, bf16[128,2048]{1,0:T(8,128)(2,1)S(1)}, u32[]{:S(2)}, u32[]{:S(2)}) %collective-permute-start.34) | collective-permute-done | bytes 524320 | tf_op jit(solution)/shard_map/ppermute | solution.py:269
  163.8 1.6 collective-permute-start.35
  165.4 9.3 %collective-permute-done.28 = bf16[128,2048]{1,0:T(8,128)(2,1)S(1)} collective-permute-done((bf16[128,2048]{1,0:T(8,128)(2,1)S(1)}, bf16[128,2048]{1,0:T(8,128)(2,1)S(1)}, u32[]{:S(2)}, u32[]{:S(2)}) %collective-permute-start.28) | collective-permute-done | bytes 524320 | tf_op jit(solution)/shard_map/ppermute | solution.py:269
  175.0 1.6 collective-permute-start.29
  177.3 8.7 %collective-permute-done.35.refs_5_ = bf16[128,2048]{1,0:T(8,128)(2,1)S(1)} collective-permute-done((bf16[128,2048]{1,0:T(8,128)(2,1)S(1)}, bf16[128,2048]{1,0:T(8,128)(2,1)S(1)}, u32[]{:S(2)}, u32[]{:S(2)}) %collective-permute-start.35) | collective-permute-done | bytes 524320 | tf_op jit(solution)/shard_map/ppermute | solution.py:269
  186.0 10.8 %collective-permute-done.29.refs_2_ = bf16[128,2048]{1,0:T(8,128)(2,1)S(1)} collective-permute-done((bf16[128,2048]{1,0:T(8,128)(2,1)S(1)}, bf16[128,2048]{1,0:T(8,128)(2,1)S(1)}, u32[]{:S(2)}, u32[]{:S(2)}) %collective-permute-start.29) | collective-permute-done | bytes 524320 | tf_op jit(solution)/shard_map/ppermute | solution.py:269
  196.8 2.0 finish.1
  (70 shorter events, 4.5 us)
Async XLA Ops:
  6.5 63.9 %all-gather.3.cloned.1.call-start = ((), (), s32[]{:S(2)}) async-start(), calls=%async_computation | async-start | bytes 2654208 | tf_op jit(solution)/shard_map/all_gather | solution.py:307
  6.6 0.9 copy-start.4
  8.1 8.3 %collective-permute-start.1 = (bf16[32,1024]{1,0:T(8,128)(2,1)S(1)}, bf16[32,1024]{1,0:T(8,128)(2,1)S(1)}, u32[]{:S(2)}, u32[]{:S(2)}) collective-permute-start(bf16[32,1024]{1,0:T(8,128)(2,1)S(1)} %get-tuple-element.49), channel_id=1, source_target_pairs={{0,8},{8,0},{16,24},{24,16},{1,9},{9,1},{17,25},{25,17},{2,10},{10... | collective-permute-start | bytes 196616 | tf_op jit(solution)/shard_map/ppermute | solution.py:275
  11.1 5.3 %collective-permute-start.2 = (bf16[32,1024]{1,0:T(8,128)(2,1)S(1)}, bf16[32,1024]{1,0:T(8,128)(2,1)S(1)}, u32[]{:S(2)}, u32[]{:S(2)}) collective-permute-start(bf16[32,1024]{1,0:T(8,128)(2,1)S(1)} %get-tuple-element.50), channel_id=1, source_target_pairs={{0,16},{8,24},{16,0},{24,8},{1,17},{9,25},{17,1},{25,9},{2,18},{10... | collective-permute-start | bytes 196616 | tf_op jit(solution)/shard_map/ppermute | solution.py:275
  12.7 5.2 %collective-permute-start.3 = (bf16[32,1024]{1,0:T(8,128)(2,1)S(1)}, bf16[32,1024]{1,0:T(8,128)(2,1)S(1)}, u32[]{:S(2)}, u32[]{:S(2)}) collective-permute-start(bf16[32,1024]{1,0:T(8,128)(2,1)S(1)} %get-tuple-element.51), channel_id=1, source_target_pairs={{0,24},{8,16},{16,8},{24,0},{1,25},{9,17},{17,9},{25,1},{2,26},{10... | collective-permute-start | bytes 196616 | tf_op jit(solution)/shard_map/ppermute | solution.py:275
  13.6 8.6 %collective-permute-start.8 = (bf16[32,4096]{1,0:T(8,128)(2,1)S(1)}, bf16[32,4096]{1,0:T(8,128)(2,1)S(1)}, u32[]{:S(2)}, u32[]{:S(2)}) collective-permute-start(bf16[32,4096]{1,0:T(8,128)(2,1)S(1)} %slice_bitcast_fusion.1), channel_id=1, source_target_pairs={{0,2},{1,3},{2,6},{3,7},{6,4},{7,5},{4,0},{5,1},{8,10},{9,11},{10,... | collective-permute-start | bytes 786440 | tf_op jit(solution)/shard_map/ppermute | solution.py:269
  17.9 4.3 %copy-start.7 = (bf16[144,1024]{1,0:T(8,128)(2,1)}, bf16[144,1024]{1,0:T(8,128)(2,1)S(1)}, u32[]{:S(2)}) copy-start(bf16[144,1024]{1,0:T(8,128)(2,1)S(1)} %constant_dynamic-update-slice_fusion) | copy-start | bytes 884740
  22.2 23.7 %collective-permute-start.4 = (bf16[1024,512]{1,0:T(8,128)(2,1)}, bf16[1024,512]{1,0:T(8,128)(2,1)S(1)}, u32[]{:S(2)}, u32[]{:S(2)}) collective-permute-start(bf16[1024,512]{1,0:T(8,128)(2,1)} %refs_0_.5), channel_id=1, source_target_pairs={{0,8},{8,0},{16,24},{24,16},{1,9},{9,1},{17,25},{25,17},{2,10},{10... | collective-permute-start | bytes 3145736 | tf_op jit(solution)/shard_map/ppermute | solution.py:275
  23.8 23.2 %collective-permute-start.5 = (bf16[1024,512]{1,0:T(8,128)(2,1)}, bf16[1024,512]{1,0:T(8,128)(2,1)S(1)}, u32[]{:S(2)}, u32[]{:S(2)}) collective-permute-start(bf16[1024,512]{1,0:T(8,128)(2,1)} %refs_0_.5), channel_id=1, source_target_pairs={{0,16},{8,24},{16,0},{24,8},{1,17},{9,25},{17,1},{25,9},{2,18},{10... | collective-permute-start | bytes 3145736 | tf_op jit(solution)/shard_map/ppermute | solution.py:275
  26.6 38.9 %collective-permute-start.15 = (bf16[96,4096]{1,0:T(8,128)(2,1)S(1)}, bf16[96,4096]{1,0:T(8,128)(2,1)S(1)}, u32[]{:S(2)}, u32[]{:S(2)}) collective-permute-start(bf16[96,4096]{1,0:T(8,128)(2,1)S(1)} %slice_bitcast_fusion), channel_id=1, source_target_pairs={{0,2},{1,3},{2,6},{3,7},{6,4},{7,5},{4,0},{5,1},{8,10},{9,11},{10,... | collective-permute-start | bytes 2359304 | tf_op jit(solution)/shard_map/ppermute | solution.py:269
  47.1 23.0 %copy-start = (bf16[1024,512]{1,0:T(8,128)(2,1)}, bf16[1024,512]{1,0:T(8,128)(2,1)S(1)}, u32[]{:S(2)}) copy-start(bf16[1024,512]{1,0:T(8,128)(2,1)S(1)} %collective-permute-done.5.refs_2_) | copy-start | bytes 3145732
  47.1 23.0 %collective-permute-start.10 = (bf16[512,1024]{1,0:T(8,128)(2,1)}, bf16[512,1024]{1,0:T(8,128)(2,1)S(1)}, u32[]{:S(2)}, u32[]{:S(2)}) collective-permute-start(bf16[512,1024]{1,0:T(8,128)(2,1)} %refs_0_.7), channel_id=1, source_target_pairs={{0,16},{8,24},{16,0},{24,8},{1,17},{9,25},{17,1},{25,9},{2,18},{10... | collective-permute-start | bytes 3145736 | tf_op jit(solution)/shard_map/ppermute | solution.py:275
  49.3 27.4 %collective-permute-start.9 = (bf16[512,1024]{1,0:T(8,128)(2,1)}, bf16[512,1024]{1,0:T(8,128)(2,1)S(1)}, u32[]{:S(2)}, u32[]{:S(2)}) collective-permute-start(bf16[512,1024]{1,0:T(8,128)(2,1)} %refs_0_.7), channel_id=1, source_target_pairs={{0,8},{8,0},{16,24},{24,16},{1,9},{9,1},{17,25},{25,17},{2,10},{10... | collective-permute-start | bytes 3145736 | tf_op jit(solution)/shard_map/ppermute | solution.py:275
  66.4 20.2 %collective-permute-start.16 = (bf16[128,4096]{1,0:T(8,128)(2,1)}, bf16[128,4096]{1,0:T(8,128)(2,1)}, u32[]{:S(2)}, u32[]{:S(2)}) collective-permute-start(bf16[128,4096]{1,0:T(8,128)(2,1)} %constant_dynamic-update-slice_fusion.5.mine), channel_id=1, source_target_pairs={{0,2},{1,3},{2,6},{3,7},{6,4},{7,5},{4,0},{5,1},{8,10},{9,11},{10,... | collective-permute-start | bytes 3145736 | tf_op jit(solution)/shard_map/ppermute | solution.py:269
  66.8 23.2 %collective-permute-start.20 = (bf16[128,4096]{1,0:T(8,128)(2,1)}, bf16[128,4096]{1,0:T(8,128)(2,1)}, u32[]{:S(2)}, u32[]{:S(2)}) collective-permute-start(bf16[128,4096]{1,0:T(8,128)(2,1)} %constant_dynamic-update-slice_fusion.5.mine), channel_id=1, source_target_pairs={{0,1},{1,0},{2,3},{3,2},{4,5},{5,4},{6,7},{7,6},{8,9},{9,8},{10,11... | collective-permute-start | bytes 3145736 | tf_op jit(solution)/shard_map/ppermute | solution.py:272
  67.7 14.7 %collective-permute-start.6 = (bf16[512,512]{1,0:T(8,128)(2,1)}, bf16[512,512]{1,0:T(8,128)(2,1)}, u32[]{:S(2)}, u32[]{:S(2)}) collective-permute-start(bf16[512,512]{1,0:T(8,128)(2,1)} %slice.32), channel_id=1, source_target_pairs={{0,16},{8,24},{16,0},{24,8},{1,17},{9,25},{17,1},{25,9},{2,18},{10... | collective-permute-start | bytes 1572872 | tf_op jit(solution)/shard_map/ppermute | solution.py:275
  70.1 15.1 %collective-permute-start.7 = (bf16[512,512]{1,0:T(8,128)(2,1)}, bf16[512,512]{1,0:T(8,128)(2,1)}, u32[]{:S(2)}, u32[]{:S(2)}) collective-permute-start(bf16[512,512]{1,0:T(8,128)(2,1)} %slice.33), channel_id=1, source_target_pairs={{0,8},{8,0},{16,24},{24,16},{1,9},{9,1},{17,25},{25,17},{2,10},{10... | collective-permute-start | bytes 1572872 | tf_op jit(solution)/shard_map/ppermute | solution.py:275
  70.4 19.6 %copy-start.1 = (bf16[1024,512]{1,0:T(8,128)(2,1)S(1)}, bf16[1024,512]{1,0:T(8,128)(2,1)}, u32[]{:S(2)}) copy-start(bf16[1024,512]{1,0:T(8,128)(2,1)} %copy-done) | copy-start | bytes 3145732
  70.4 19.6 %copy-start.2 = (bf16[1024,512]{1,0:T(8,128)(2,1)S(1)}, bf16[1024,512]{1,0:T(8,128)(2,1)}, u32[]{:S(2)}) copy-start(bf16[1024,512]{1,0:T(8,128)(2,1)} %refs_0_.5) | copy-start | bytes 3145732
  76.7 19.6 %collective-permute-start.11 = (bf16[256,1024]{1,0:T(8,128)(2,1)}, bf16[256,1024]{1,0:T(8,128)(2,1)S(1)}, u32[]{:S(2)}, u32[]{:S(2)}) collective-permute-start(bf16[256,1024]{1,0:T(8,128)(2,1)} %get-tuple-element.65), channel_id=1, source_target_pairs={{0,8},{8,0},{16,24},{24,16},{1,9},{9,1},{17,25},{25,17},{2,10},{10... | collective-permute-start | bytes 1572872 | tf_op jit(solution)/shard_map/ppermute | solution.py:275
  82.3 25.2 %collective-permute-start.12 = (bf16[256,1024]{1,0:T(8,128)(2,1)}, bf16[256,1024]{1,0:T(8,128)(2,1)S(1)}, u32[]{:S(2)}, u32[]{:S(2)}) collective-permute-start(bf16[256,1024]{1,0:T(8,128)(2,1)} %get-tuple-element.66), channel_id=1, source_target_pairs={{0,16},{8,24},{16,0},{24,8},{1,17},{9,25},{17,1},{25,9},{2,18},{10... | collective-permute-start | bytes 1572872 | tf_op jit(solution)/shard_map/ppermute | solution.py:275
  85.1 24.1 %collective-permute-start.13 = (bf16[256,1024]{1,0:T(8,128)(2,1)}, bf16[256,1024]{1,0:T(8,128)(2,1)S(1)}, u32[]{:S(2)}, u32[]{:S(2)}) collective-permute-start(bf16[256,1024]{1,0:T(8,128)(2,1)} %get-tuple-element.67), channel_id=1, source_target_pairs={{0,24},{8,16},{16,8},{24,0},{1,25},{9,17},{17,9},{25,1},{2,26},{10... | collective-permute-start | bytes 1572872 | tf_op jit(solution)/shard_map/ppermute | solution.py:275
  86.6 32.7 %collective-permute-start.17 = (bf16[128,4096]{1,0:T(8,128)(2,1)}, bf16[128,4096]{1,0:T(8,128)(2,1)S(1)}, u32[]{:S(2)}, u32[]{:S(2)}) collective-permute-start(bf16[128,4096]{1,0:T(8,128)(2,1)} %collective-permute-done.16.mine), channel_id=1, source_target_pairs={{0,2},{1,3},{2,6},{3,7},{6,4},{7,5},{4,0},{5,1},{8,10},{9,11},{10,... | collective-permute-start | bytes 3145736 | tf_op jit(solution)/shard_map/ppermute | solution.py:269
  90.0 33.5 %collective-permute-start.24 = (bf16[128,4096]{1,0:T(8,128)(2,1)}, bf16[128,4096]{1,0:T(8,128)(2,1)S(1)}, u32[]{:S(2)}, u32[]{:S(2)}) collective-permute-start(bf16[128,4096]{1,0:T(8,128)(2,1)} %collective-permute-done.16.mine), channel_id=1, source_target_pairs={{0,1},{1,0},{2,3},{3,2},{4,5},{5,4},{6,7},{7,6},{8,9},{9,8},{10,11... | collective-permute-start | bytes 3145736 | tf_op jit(solution)/shard_map/ppermute | solution.py:272
  93.5 15.7 %copy-start.6 = (f32[256,1024]{1,0:T(8,128)S(1)}, f32[256,1024]{1,0:T(8,128)}, u32[]{:S(2)}) copy-start(f32[256,1024]{1,0:T(8,128)} %get-tuple-element.64) | copy-start | bytes 3145732
  93.6 16.0 %copy-start.5 = (f32[8,256]{1,0:T(8,128)S(1)}, f32[8,256]{1,0:T(8,128)}, u32[]{:S(2)}) copy-start(f32[8,256]{1,0:T(8,128)} %get-tuple-element.58.open_ref) | copy-start | bytes 24580
  96.3 22.3 %collective-permute-start.21 = (bf16[256,1024]{1,0:T(8,128)(2,1)S(1)}, bf16[256,1024]{1,0:T(8,128)(2,1)S(1)}, u32[]{:S(2)}, u32[]{:S(2)}) collective-permute-start(bf16[256,1024]{1,0:T(8,128)(2,1)S(1)} %slice.30), channel_id=1, source_target_pairs={{0,16},{8,24},{16,0},{24,8},{1,17},{9,25},{17,1},{25,9},{2,18},{10... | collective-permute-start | bytes 1572872 | tf_op jit(solution)/shard_map/ppermute | solution.py:275
  107.5 11.0 %collective-permute-start.22 = (bf16[256,1024]{1,0:T(8,128)(2,1)S(1)}, bf16[256,1024]{1,0:T(8,128)(2,1)S(1)}, u32[]{:S(2)}, u32[]{:S(2)}) collective-permute-start(bf16[256,1024]{1,0:T(8,128)(2,1)S(1)} %slice.31), channel_id=1, source_target_pairs={{0,8},{8,0},{16,24},{24,16},{1,9},{9,1},{17,25},{25,17},{2,10},{10... | collective-permute-start | bytes 1572872 | tf_op jit(solution)/shard_map/ppermute | solution.py:275
  113.8 6.1 %collective-permute-start.25 = (bf16[128,2048]{1,0:T(8,128)(2,1)S(1)}, bf16[128,2048]{1,0:T(8,128)(2,1)S(1)}, u32[]{:S(2)}, u32[]{:S(2)}) collective-permute-start(bf16[128,2048]{1,0:T(8,128)(2,1)S(1)} %get-tuple-element.79), channel_id=1, source_target_pairs={{0,1},{1,0},{2,3},{3,2},{4,5},{5,4},{6,7},{7,6},{8,9},{9,8},{10,11... | collective-permute-start | bytes 1572872 | tf_op jit(solution)/shard_map/ppermute | solution.py:272
  119.3 7.4 %collective-permute-start.23 = (bf16[128,2048]{1,0:T(8,128)(2,1)S(1)}, bf16[128,2048]{1,0:T(8,128)(2,1)S(1)}, u32[]{:S(2)}, u32[]{:S(2)}) collective-permute-start(bf16[128,2048]{1,0:T(8,128)(2,1)S(1)} %get-tuple-element.76), channel_id=1, source_target_pairs={{0,1},{1,0},{2,3},{3,2},{4,5},{5,4},{6,7},{7,6},{8,9},{9,8},{10,11... | collective-permute-start | bytes 1572872 | tf_op jit(solution)/shard_map/ppermute | solution.py:272
  119.4 19.8 %collective-permute-start.18 = (bf16[128,4096]{1,0:T(8,128)(2,1)S(1)}, bf16[128,4096]{1,0:T(8,128)(2,1)S(1)}, u32[]{:S(2)}, u32[]{:S(2)}) collective-permute-start(bf16[128,4096]{1,0:T(8,128)(2,1)S(1)} %collective-permute-done.17.mine), channel_id=1, source_target_pairs={{0,1},{1,0},{2,3},{3,2},{4,5},{5,4},{6,7},{7,6},{8,9},{9,8},{10,11... | collective-permute-start | bytes 3145736 | tf_op jit(solution)/shard_map/ppermute | solution.py:272
  120.0 15.8 %collective-permute-start.26 = (bf16[128,2048]{1,0:T(8,128)(2,1)S(1)}, bf16[128,2048]{1,0:T(8,128)(2,1)S(1)}, u32[]{:S(2)}, u32[]{:S(2)}) collective-permute-start(bf16[128,2048]{1,0:T(8,128)(2,1)S(1)} %add_convert_fusion.4), channel_id=1, source_target_pairs={{0,2},{1,3},{2,6},{3,7},{6,4},{7,5},{4,0},{5,1},{8,10},{9,11},{10,... | collective-permute-start | bytes 1572872 | tf_op jit(solution)/shard_map/ppermute | solution.py:269
  126.7 9.9 %copy-start.3 = (bf16[1,1,128,4096]{3,2,1,0:T(8,128)(2,1)S(1)}, bf16[1,1,128,4096]{3,2,1,0:T(8,128)(2,1)}, u32[]{:S(2)}) copy-start(bf16[1,1,128,4096]{3,2,1,0:T(8,128)(2,1)} %param.8) | copy-start | bytes 3145732
  129.1 18.4 %collective-permute-start.33 = (bf16[128,2048]{1,0:T(8,128)(2,1)S(1)}, bf16[128,2048]{1,0:T(8,128)(2,1)S(1)}, u32[]{:S(2)}, u32[]{:S(2)}) collective-permute-start(bf16[128,2048]{1,0:T(8,128)(2,1)S(1)} %add_convert_fusion.5), channel_id=1, source_target_pairs={{0,2},{1,3},{2,6},{3,7},{6,4},{7,5},{4,0},{5,1},{8,10},{9,11},{10,... | collective-permute-start | bytes 1572872 | tf_op jit(solution)/shard_map/ppermute | solution.py:269
  136.5 11.1 %collective-permute-start.32 = (bf16[128,2048]{1,0:T(8,128)(2,1)S(1)}, bf16[128,2048]{1,0:T(8,128)(2,1)S(1)}, u32[]{:S(2)}, u32[]{:S(2)}) collective-permute-start(bf16[128,2048]{1,0:T(8,128)(2,1)S(1)} %get-tuple-element.89), channel_id=1, source_target_pairs={{0,1},{1,0},{2,3},{3,2},{4,5},{5,4},{6,7},{7,6},{8,9},{9,8},{10,11... | collective-permute-start | bytes 1572872 | tf_op jit(solution)/shard_map/ppermute | solution.py:272
  136.6 14.9 %collective-permute-start = (bf16[128,4096]{1,0:T(8,128)(2,1)S(1)}, bf16[128,4096]{1,0:T(8,128)(2,1)S(1)}, u32[]{:S(2)}, u32[]{:S(2)}) collective-permute-start(bf16[128,4096]{1,0:T(8,128)(2,1)S(1)} %bitcast.15), channel_id=1, source_target_pairs={{0,1},{1,0},{2,3},{3,2},{4,5},{5,4},{6,7},{7,6},{8,9},{9,8},{10,11... | collective-permute-start | bytes 3145736 | tf_op jit(solution)/shard_map/ppermute | solution.py:272
  139.0 11.4 %collective-permute-start.27 = (bf16[128,2048]{1,0:T(8,128)(2,1)S(1)}, bf16[128,2048]{1,0:T(8,128)(2,1)S(1)}, u32[]{:S(2)}, u32[]{:S(2)}) collective-permute-start(bf16[128,2048]{1,0:T(8,128)(2,1)S(1)} %get-tuple-element.82), channel_id=1, source_target_pairs={{0,1},{1,0},{2,3},{3,2},{4,5},{5,4},{6,7},{7,6},{8,9},{9,8},{10,11... | collective-permute-start | bytes 1572872 | tf_op jit(solution)/shard_map/ppermute | solution.py:272
  147.0 12.5 %collective-permute-start.31 = (bf16[128,2048]{1,0:T(8,128)(2,1)S(1)}, bf16[128,2048]{1,0:T(8,128)(2,1)S(1)}, u32[]{:S(2)}, u32[]{:S(2)}) collective-permute-start(bf16[128,2048]{1,0:T(8,128)(2,1)S(1)} %get-tuple-element.87), channel_id=1, source_target_pairs={{0,1},{1,0},{2,3},{3,2},{4,5},{5,4},{6,7},{7,6},{8,9},{9,8},{10,11... | collective-permute-start | bytes 1572872 | tf_op jit(solution)/shard_map/ppermute | solution.py:272
  147.5 17.9 %collective-permute-start.19 = (bf16[128,2048]{1,0:T(8,128)(2,1)S(1)}, bf16[128,2048]{1,0:T(8,128)(2,1)S(1)}, u32[]{:S(2)}, u32[]{:S(2)}) collective-permute-start(bf16[128,2048]{1,0:T(8,128)(2,1)S(1)} %get-tuple-element.73), channel_id=1, source_target_pairs={{0,1},{1,0},{2,3},{3,2},{4,5},{5,4},{6,7},{7,6},{8,9},{9,8},{10,11... | collective-permute-start | bytes 1572872 | tf_op jit(solution)/shard_map/ppermute | solution.py:272
  147.8 15.7 %collective-permute-start.34 = (bf16[128,2048]{1,0:T(8,128)(2,1)S(1)}, bf16[128,2048]{1,0:T(8,128)(2,1)S(1)}, u32[]{:S(2)}, u32[]{:S(2)}) collective-permute-start(bf16[128,2048]{1,0:T(8,128)(2,1)S(1)} %add_convert_fusion.1), channel_id=1, source_target_pairs={{0,2},{1,3},{2,6},{3,7},{6,4},{7,5},{4,0},{5,1},{8,10},{9,11},{10,... | collective-permute-start | bytes 1572872 | tf_op jit(solution)/shard_map/ppermute | solution.py:269
  150.6 24.1 %collective-permute-start.28 = (bf16[128,2048]{1,0:T(8,128)(2,1)S(1)}, bf16[128,2048]{1,0:T(8,128)(2,1)S(1)}, u32[]{:S(2)}, u32[]{:S(2)}) collective-permute-start(bf16[128,2048]{1,0:T(8,128)(2,1)S(1)} %add_convert_fusion.3), channel_id=1, source_target_pairs={{0,2},{1,3},{2,6},{3,7},{6,4},{7,5},{4,0},{5,1},{8,10},{9,11},{10,... | collective-permute-start | bytes 1572872 | tf_op jit(solution)/shard_map/ppermute | solution.py:269
  159.4 17.9 %collective-permute-start.30 = (bf16[128,2048]{1,0:T(8,128)(2,1)S(1)}, bf16[128,2048]{1,0:T(8,128)(2,1)S(1)}, u32[]{:S(2)}, u32[]{:S(2)}) collective-permute-start(bf16[128,2048]{1,0:T(8,128)(2,1)S(1)} %get-tuple-element.85), channel_id=1, source_target_pairs={{0,1},{1,0},{2,3},{3,2},{4,5},{5,4},{6,7},{7,6},{8,9},{9,8},{10,11... | collective-permute-start | bytes 1572872 | tf_op jit(solution)/shard_map/ppermute | solution.py:272
  159.5 17.8 %collective-permute-start.14 = (bf16[128,2048]{1,0:T(8,128)(2,1)S(1)}, bf16[128,2048]{1,0:T(8,128)(2,1)S(1)}, u32[]{:S(2)}, u32[]{:S(2)}) collective-permute-start(bf16[128,2048]{1,0:T(8,128)(2,1)S(1)} %get-tuple-element.70), channel_id=1, source_target_pairs={{0,1},{1,0},{2,3},{3,2},{4,5},{5,4},{6,7},{7,6},{8,9},{9,8},{10,11... | collective-permute-start | bytes 1572872 | tf_op jit(solution)/shard_map/ppermute | solution.py:272
  163.8 22.2 %collective-permute-start.35 = (bf16[128,2048]{1,0:T(8,128)(2,1)S(1)}, bf16[128,2048]{1,0:T(8,128)(2,1)S(1)}, u32[]{:S(2)}, u32[]{:S(2)}) collective-permute-start(bf16[128,2048]{1,0:T(8,128)(2,1)S(1)} %add_convert_fusion), channel_id=1, source_target_pairs={{0,2},{1,3},{2,6},{3,7},{6,4},{7,5},{4,0},{5,1},{8,10},{9,11},{10,... | collective-permute-start | bytes 1572872 | tf_op jit(solution)/shard_map/ppermute | solution.py:269
  175.0 21.8 %collective-permute-start.29 = (bf16[128,2048]{1,0:T(8,128)(2,1)S(1)}, bf16[128,2048]{1,0:T(8,128)(2,1)S(1)}, u32[]{:S(2)}, u32[]{:S(2)}) collective-permute-start(bf16[128,2048]{1,0:T(8,128)(2,1)S(1)} %add_convert_fusion.2), channel_id=1, source_target_pairs={{0,2},{1,3},{2,6},{3,7},{6,4},{7,5},{4,0},{5,1},{8,10},{9,11},{10,... | collective-permute-start | bytes 1572872 | tf_op jit(solution)/shard_map/ppermute | solution.py:269
Sparse Core Ops, SparseCore 0:
  22.4 43.5 all-gather.2
where the time goes:
time: 206 us
  waiting for transfers between devices  103 us (50%)
  Pallas kernels  40.9 us (20%)
  starting transfers between devices  38.5 us (19%)
  between operations  14.4 us (7%)
  local copies, waits for them, and re-layouts  6.73 us (3%)
  other arithmetic  2.3 us (1%)
    ppermute x10, waiting for transfers between devices, to_next(): return lax.ppermute(value, 'cand', along)  58.7 us
    ppermute x14, waiting for transfers between devices, flip(): return lax.ppermute(value, 'prod', [(q, q ^ r) for q in range(parts)])  43.9 us
    ppermute x14, starting transfers between devices, flip(): return lax.ppermute(value, 'prod', [(q, q ^ r) for q in range(parts)])  18.8 us
    ppermute x10, starting transfers between devices, to_next(): return lax.ppermute(value, 'cand', along)  17.2 us
    pallas_call x4, Pallas kernels, query(): pl.pallas_call(functools.partial(query_kernel, len(weights), parts), out_...  12.5 us
    pallas_call x8, Pallas kernels, project(): pl.pallas_call(functools.partial(project_kernel, pieces), out_shape=[shap...  10.6 us
    pallas_call x4, Pallas kernels, attend(): pl.pallas_call(functools.partial(attend_kernel, order, step), out_shape=j...  9 us
    pallas_call x1, Pallas kernels, key_value(): pl.pallas_call(functools.partial(key_value_kernel, parts, rows, tiles), o...  6.27 us
  transfers between devices with their start and end apart: 37, of which 15 were waited for; matrix products, arithmetic and copies ran while one was open for 4% of the time, Pallas kernels for 19%

commit v1 on v0

--- a/solution.py
+++ b/solution.py
@@ -291,7 +291,7 @@
     clen, width = cand_states.shape[2:]
     states = cand_states.reshape(clen, width)
     pairs = [(states, to_sib(states))]
-    cut = clen // 4
+    cut = clen // 8
     top = to_next(states[:cut])
 
     rows = enc_rows.shape[1]

time: 206 us -> 206 us (level)
  starting transfers between devices: 38.5 us -> 34.2 us
  waiting for transfers between devices: 103 us -> 107 us
    ppermute x10, starting transfers between devices: 17.2 us -> 14.7 us  [to_next(): return lax.ppermute(value, 'cand', along)]
    ppermute x10, waiting for transfers between devices: 58.7 us -> 60.8 us  [to_next(): return lax.ppermute(value, 'cand', along)]
    ppermute x14, waiting for transfers between devices: 43.9 us -> 46 us  [flip(): return lax.ppermute(value, 'prod', [(q, q ^ r) for q in range(parts)])]
  transfers between devices with their start and end apart: 37 -> 37, of which waited for: 15 -> 16; matrix products, arithmetic and copies ran while one was open for 4% -> 4% of each run, Pallas kernels for 19% -> 19%
where the time goes in v1:
time: 206 us
  waiting for transfers between devices  107 us (52%)
  Pallas kernels  40.9 us (20%)
  starting transfers between devices  34.2 us (17%)
  between operations  14.4 us (7%)
  local copies, waits for them, and re-layouts  6.75 us (3%)
  other arithmetic  2.3 us (1%)
    ppermute x10, waiting for transfers between devices, to_next(): return lax.ppermute(value, 'cand', along)  60.8 us
    ppermute x14, waiting for transfers between devices, flip(): return lax.ppermute(value, 'prod', [(q, q ^ r) for q in range(parts)])  46 us
    ppermute x14, starting transfers between devices, flip(): return lax.ppermute(value, 'prod', [(q, q ^ r) for q in range(parts)])  17 us
    ppermute x10, starting transfers between devices, to_next(): return lax.ppermute(value, 'cand', along)  14.7 us
    pallas_call x4, Pallas kernels, query(): pl.pallas_call(functools.partial(query_kernel, len(weights), parts), out_...  12.5 us
    pallas_call x8, Pallas kernels, project(): pl.pallas_call(functools.partial(project_kernel, pieces), out_shape=[shap...  10.6 us
    pallas_call x4, Pallas kernels, attend(): pl.pallas_call(functools.partial(attend_kernel, order, step), out_shape=j...  9 us
    pallas_call x1, Pallas kernels, key_value(): pl.pallas_call(functools.partial(key_value_kernel, parts, rows, tiles), o...  6.28 us
  transfers between devices with their start and end apart: 37, of which 16 were waited for; matrix products, arithmetic and copies ran while one was open for 4% of the time, Pallas kernels for 19%

profile of v1, /device:TPU:0, one launch (start us, length us, event | category | flops | bytes accessed | tf_op | source)
XLA Modules:
  0.0 205.5 jit_solution(5559760458053901900)
XLA Ops:
  6.6 0.9 copy-done.4
  7.6 0.6 columns.1
  8.1 3.0 %collective-permute-start.1 = (bf16[32,1024]{1,0:T(8,128)(2,1)S(1)}, bf16[32,1024]{1,0:T(8,128)(2,1)S(1)}, u32[]{:S(2)}, u32[]{:S(2)}) collective-permute-start(bf16[32,1024]{1,0:T(8,128)(2,1)S(1)} %get-tuple-element.49), channel_id=1, source_target_pairs={{0,8},{8,0},{16,24},{24,16},{1,9},{9,1},{17,25},{25,17},{2,10},{10... | collective-permute-start | bytes 196616 | tf_op jit(solution)/shard_map/ppermute | solution.py:275
  11.1 1.5 collective-permute-start.2
  12.7 0.9 slice_bitcast_fusion.1
  13.6 2.1 %collective-permute-start.8 = (bf16[16,4096]{1,0:T(8,128)(2,1)S(1)}, bf16[16,4096]{1,0:T(8,128)(2,1)S(1)}, u32[]{:S(2)}, u32[]{:S(2)}) collective-permute-start(bf16[16,4096]{1,0:T(8,128)(2,1)S(1)} %slice_bitcast_fusion.1), channel_id=1, source_target_pairs={{0,2},{1,3},{2,6},{3,7},{6,4},{7,5},{4,0},{5,1},{8,10},{9,11},{10,... | collective-permute-start | bytes 393224 | tf_op jit(solution)/shard_map/ppermute | solution.py:269
  15.7 0.7 convert_bitcast_fusion
  16.4 1.4 collective-permute-done.3
  17.9 1.7 collective-permute-done.8
  19.7 1.9 collective-permute-start.4
  21.6 1.5 collective-permute-start.5
  23.1 1.2 slice_bitcast_fusion
  24.3 0.9 collective-permute-start.15
  25.2 18.1 %collective-permute-done.4.refs_1_ = bf16[1024,512]{1,0:T(8,128)(2,1)S(1)} collective-permute-done((bf16[1024,512]{1,0:T(8,128)(2,1)}, bf16[1024,512]{1,0:T(8,128)(2,1)S(1)}, u32[]{:S(2)}, u32[]{:S(2)}) %collective-permute-start.4) | collective-permute-done | bytes 1048608 | tf_op jit(solution)/shard_map/ppermute | solution.py:275
  43.3 1.5 collective-permute-done.5.refs_2_
  44.8 1.5 collective-permute-start.10
  46.3 0.7 constant_dynamic-update-slice_fusion.6
  47.0 0.5 collective-permute-start.9
  47.5 18.3 %collective-permute-done.15 = bf16[112,4096]{1,0:T(8,128)(2,1)S(1)} collective-permute-done((bf16[112,4096]{1,0:T(8,128)(2,1)S(1)}, bf16[112,4096]{1,0:T(8,128)(2,1)S(1)}, u32[]{:S(2)}, u32[]{:S(2)}) %collective-permute-start.15) | collective-permute-done | bytes 917536 | tf_op jit(solution)/shard_map/ppermute | solution.py:269
  65.8 1.0 constant_dynamic-update-slice_fusion.5.mine
  66.8 0.9 slice.32
  67.7 0.7 collective-permute-start.6
  68.4 0.9 slice.33
  69.3 0.8 collective-permute-start.7
  70.1 6.3 %key_value.1 = (f32[8,256]{1,0:T(8,128)}, f32[256,1024]{1,0:T(8,128)}, bf16[256,1024]{1,0:T(8,128)(2,1)}, bf16[256,1024]{1,0:T(8,128)(2,1)}, bf16[256,1024]{1,0:T(8,128)(2,1)}) custom-call(bf16[8,144,1024]{2,1,0:T(8,128)(2,1)} %bitcast.19, bf16[1024,512]{1,0:T(8,128)(2,1)} %w_key.1, bf16[1024,512]{1,0:T(8,128)(2,1)} %w_value.1), custom_call_target="tpu_custom_call" | custom-call | flops 3000000000 | bytes 1 | tf_op jit(solution)/shard_map/key_value/pallas_call | solution.py:76
  76.3 1.3 collective-permute-start.11
  77.6 4.7 %collective-permute-done.6.refs_3_ = bf16[512,512]{1,0:T(8,128)(2,1)} collective-permute-done((bf16[512,512]{1,0:T(8,128)(2,1)}, bf16[512,512]{1,0:T(8,128)(2,1)}, u32[]{:S(2)}, u32[]{:S(2)}) %collective-permute-start.6) | collective-permute-done | bytes 524320 | tf_op jit(solution)/shard_map/ppermute | solution.py:275
  82.3 0.7 collective-permute-start.12
  83.1 1.3 collective-permute-done.7.refs_4_
  84.4 1.5 collective-permute-start.13
  85.9 0.5 collective-permute-done.16.mine
  86.4 2.9 %collective-permute-start.17 = (bf16[128,4096]{1,0:T(8,128)(2,1)}, bf16[128,4096]{1,0:T(8,128)(2,1)S(1)}, u32[]{:S(2)}, u32[]{:S(2)}) collective-permute-start(bf16[128,4096]{1,0:T(8,128)(2,1)} %collective-permute-done.16.mine), channel_id=1, source_target_pairs={{0,2},{1,3},{2,6},{3,7},{6,4},{7,5},{4,0},{5,1},{8,10},{9,11},{10,... | collective-permute-start | bytes 3145736 | tf_op jit(solution)/shard_map/ppermute | solution.py:269
  89.3 3.5 %query.6.query_ref = bf16[256,512]{1,0:T(8,128)(2,1)S(1)} custom-call(s32[2]{0:T(128)S(1)} %pad_add_fusion.ids, bf16[128,4096]{1,0:T(8,128)(2,1)} %constant_dynamic-update-slice_fusion.5.mine, bf16[128,4096]{1,0:T(8,128)(2,1)} %collective-permute-done.20.sib, bf16[1024,512]{1,0:T(8,128)(2,1)S(1)} %copy-done.2, ...), custom_call_target="tpu_custom_call" | custom-call | flops 1 | bytes 1 | tf_op jit(solution)/shard_map/query/pallas_call | solution.py:119
  92.9 2.6 %collective-permute-done.11 = bf16[256,1024]{1,0:T(8,128)(2,1)S(1)} collective-permute-done((bf16[256,1024]{1,0:T(8,128)(2,1)}, bf16[256,1024]{1,0:T(8,128)(2,1)S(1)}, u32[]{:S(2)}, u32[]{:S(2)}) %collective-permute-start.11) | collective-permute-done | bytes 524320 | tf_op jit(solution)/shard_map/ppermute | solution.py:275
  95.5 1.3 collective-permute-start.21
  96.8 10.9 %collective-permute-done.12 = bf16[256,1024]{1,0:T(8,128)(2,1)S(1)} collective-permute-done((bf16[256,1024]{1,0:T(8,128)(2,1)}, bf16[256,1024]{1,0:T(8,128)(2,1)S(1)}, u32[]{:S(2)}, u32[]{:S(2)}) %collective-permute-start.12) | collective-permute-done | bytes 524320 | tf_op jit(solution)/shard_map/ppermute | solution.py:275
  107.7 0.8 collective-permute-start.22
  108.8 2.2 %attend.6.context_ref = bf16[256,512]{1,0:T(8,128)(2,1)S(1)} custom-call(s32[2]{0:T(128)S(1)} %pad_add_fusion.ids, bf16[256,512]{1,0:T(8,128)(2,1)S(1)} %query.6.query_ref, f32[8,256]{1,0:T(8,128)S(1)} %copy-done.5, bf16[256,1024]{1,0:T(8,128)(2,1)S(1)} %add_convert_fusion.6.kv_ref), custom_call_target="tpu_custom_call" | custom-call | flops 1 | bytes 1 | tf_op jit(solution)/shard_map/attend/pallas_call | solution.py:179
  111.1 1.9 project.11
  113.1 5.5 %collective-permute-done.21.refs_1_ = bf16[256,1024]{1,0:T(8,128)(2,1)S(1)} collective-permute-done((bf16[256,1024]{1,0:T(8,128)(2,1)S(1)}, bf16[256,1024]{1,0:T(8,128)(2,1)S(1)}, u32[]{:S(2)}, u32[]{:S(2)}) %collective-permute-start.21) | collective-permute-done | bytes 524320 | tf_op jit(solution)/shard_map/ppermute | solution.py:275
  118.6 0.7 project.10
  120.0 3.0 %collective-permute-start.26 = (bf16[128,2048]{1,0:T(8,128)(2,1)S(1)}, bf16[128,2048]{1,0:T(8,128)(2,1)S(1)}, u32[]{:S(2)}, u32[]{:S(2)}) collective-permute-start(bf16[128,2048]{1,0:T(8,128)(2,1)S(1)} %add_convert_fusion.4), channel_id=1, source_target_pairs={{0,2},{1,3},{2,6},{3,7},{6,4},{7,5},{4,0},{5,1},{8,10},{9,11},{10,... | collective-permute-start | bytes 1572872 | tf_op jit(solution)/shard_map/ppermute | solution.py:269
  123.1 3.2 %query.7.query_ref = bf16[256,512]{1,0:T(8,128)(2,1)S(1)} custom-call(s32[2]{0:T(128)S(1)} %pad_add_fusion.ids, bf16[128,4096]{1,0:T(8,128)(2,1)} %collective-permute-done.16.mine, bf16[128,4096]{1,0:T(8,128)(2,1)S(1)} %collective-permute-done.24.sib, bf16[1024,512]{1,0:T(8,128)(2,1)S(1)} %copy-done.2, bf16[1024,512]{1,0:T(8,128)(2,1)S(1)} %collective-permute-done.4.refs_1_, ...), custom_call_target="tpu_custom_call" | custom-call | flops 1 | bytes 1 | tf_op jit(solution)/shard_map/query/pallas_call | solution.py:119
  126.4 2.3 %attend.7.context_ref = bf16[256,512]{1,0:T(8,128)(2,1)S(1)} custom-call(s32[2]{0:T(128)S(1)} %pad_add_fusion.ids, bf16[256,512]{1,0:T(8,128)(2,1)S(1)} %query.7.query_ref, f32[8,256]{1,0:T(8,128)S(1)} %copy-done.5, bf16[256,1024]{1,0:T(8,128)(2,1)S(1)} %add_convert_fusion.6.kv_ref), custom_call_target="tpu_custom_call" | custom-call | flops 1 | bytes 1 | tf_op jit(solution)/shard_map/attend/pallas_call | solution.py:179
  128.9 6.8 %collective-permute-done.26 = bf16[128,2048]{1,0:T(8,128)(2,1)S(1)} collective-permute-done((bf16[128,2048]{1,0:T(8,128)(2,1)S(1)}, bf16[128,2048]{1,0:T(8,128)(2,1)S(1)}, u32[]{:S(2)}, u32[]{:S(2)}) %collective-permute-start.26) | collective-permute-done | bytes 524320 | tf_op jit(solution)/shard_map/ppermute | solution.py:269
  135.7 0.7 project.15
  137.0 1.9 project.12
  139.1 2.9 %query.5.query_ref = bf16[256,512]{1,0:T(8,128)(2,1)S(1)} custom-call(s32[2]{0:T(128)S(1)} %pad_add_fusion.ids, bf16[128,4096]{1,0:T(8,128)(2,1)S(1)} %collective-permute-done.17.mine, bf16[128,4096]{1,0:T(8,128)(2,1)S(1)} %collective-permute-done.18.sib, bf16[1024,512]{1,0:T(8,128)(2,1)S(1)} %copy-done.2, ...), custom_call_target="tpu_custom_call" | custom-call | flops 1 | bytes 1 | tf_op jit(solution)/shard_map/query/pallas_call | solution.py:119
  142.0 2.3 %attend.5.context_ref = bf16[256,512]{1,0:T(8,128)(2,1)S(1)} custom-call(s32[2]{0:T(128)S(1)} %pad_add_fusion.ids, bf16[256,512]{1,0:T(8,128)(2,1)S(1)} %query.5.query_ref, f32[8,256]{1,0:T(8,128)S(1)} %copy-done.5, bf16[256,1024]{1,0:T(8,128)(2,1)S(1)} %add_convert_fusion.6.kv_ref), custom_call_target="tpu_custom_call" | custom-call | flops 1 | bytes 1 | tf_op jit(solution)/shard_map/attend/pallas_call | solution.py:179
  144.3 1.9 project.9
  146.2 0.7 project.14
  147.8 2.2 %collective-permute-start.34 = (bf16[128,2048]{1,0:T(8,128)(2,1)S(1)}, bf16[128,2048]{1,0:T(8,128)(2,1)S(1)}, u32[]{:S(2)}, u32[]{:S(2)}) collective-permute-start(bf16[128,2048]{1,0:T(8,128)(2,1)S(1)} %add_convert_fusion.1), channel_id=1, source_target_pairs={{0,2},{1,3},{2,6},{3,7},{6,4},{7,5},{4,0},{5,1},{8,10},{9,11},{10,... | collective-permute-start | bytes 1572872 | tf_op jit(solution)/shard_map/ppermute | solution.py:269
  150.2 0.9 collective-permute-start.28
  151.1 2.9 %query.4.query_ref = bf16[256,512]{1,0:T(8,128)(2,1)S(1)} custom-call(s32[2]{0:T(128)S(1)} %pad_add_fusion.ids, bf16[128,4096]{1,0:T(8,128)(2,1)S(1)} %bitcast.16, bf16[128,4096]{1,0:T(8,128)(2,1)S(1)} %collective-permute-done.sib, bf16[1024,512]{1,0:T(8,128)(2,1)S(1)} %copy-done.2, bf16[1024,512]{1,0:T(8,128)(2,1)S(1)} %collective-permute-done.4.refs_1_, ...), custom_call_target="tpu_custom_call" | custom-call | flops 1 | bytes 1 | tf_op jit(solution)/shard_map/query/pallas_call | solution.py:119
  154.0 2.2 %attend.4.context_ref = bf16[256,512]{1,0:T(8,128)(2,1)S(1)} custom-call(s32[2]{0:T(128)S(1)} %pad_add_fusion.ids, bf16[256,512]{1,0:T(8,128)(2,1)S(1)} %query.4.query_ref, f32[8,256]{1,0:T(8,128)S(1)} %copy-done.5, bf16[256,1024]{1,0:T(8,128)(2,1)S(1)} %add_convert_fusion.6.kv_ref), custom_call_target="tpu_custom_call" | custom-call | flops 1 | bytes 1 | tf_op jit(solution)/shard_map/attend/pallas_call | solution.py:179
  156.3 1.9 project.8
  158.2 0.7 project.13
  159.5 3.9 %collective-permute-done.34 = bf16[128,2048]{1,0:T(8,128)(2,1)S(1)} collective-permute-done((bf16[128,2048]{1,0:T(8,128)(2,1)S(1)}, bf16[128,2048]{1,0:T(8,128)(2,1)S(1)}, u32[]{:S(2)}, u32[]{:S(2)}) %collective-permute-start.34) | collective-permute-done | bytes 524320 | tf_op jit(solution)/shard_map/ppermute | solution.py:269
  163.7 1.3 collective-permute-start.35
  165.0 9.7 %collective-permute-done.28 = bf16[128,2048]{1,0:T(8,128)(2,1)S(1)} collective-permute-done((bf16[128,2048]{1,0:T(8,128)(2,1)S(1)}, bf16[128,2048]{1,0:T(8,128)(2,1)S(1)}, u32[]{:S(2)}, u32[]{:S(2)}) %collective-permute-start.28) | collective-permute-done | bytes 524320 | tf_op jit(solution)/shard_map/ppermute | solution.py:269
  174.9 1.3 collective-permute-start.29
  176.9 9.1 %collective-permute-done.35.refs_5_ = bf16[128,2048]{1,0:T(8,128)(2,1)S(1)} collective-permute-done((bf16[128,2048]{1,0:T(8,128)(2,1)S(1)}, bf16[128,2048]{1,0:T(8,128)(2,1)S(1)}, u32[]{:S(2)}, u32[]{:S(2)}) %collective-permute-start.35) | collective-permute-done | bytes 524320 | tf_op jit(solution)/shard_map/ppermute | solution.py:269
  185.9 10.8 %collective-permute-done.29.refs_2_ = bf16[128,2048]{1,0:T(8,128)(2,1)S(1)} collective-permute-done((bf16[128,2048]{1,0:T(8,128)(2,1)S(1)}, bf16[128,2048]{1,0:T(8,128)(2,1)S(1)}, u32[]{:S(2)}, u32[]{:S(2)}) %collective-permute-start.29) | collective-permute-done | bytes 524320 | tf_op jit(solution)/shard_map/ppermute | solution.py:269
  196.7 2.0 finish.1
  (70 shorter events, 4.7 us)
Async XLA Ops:
  6.5 63.5 %all-gather.3.cloned.1.call-start = ((), (), s32[]{:S(2)}) async-start(), calls=%async_computation | async-start | bytes 2654208 | tf_op jit(solution)/shard_map/all_gather | solution.py:307
  6.6 0.9 copy-start.4
  8.1 8.3 %collective-permute-start.1 = (bf16[32,1024]{1,0:T(8,128)(2,1)S(1)}, bf16[32,1024]{1,0:T(8,128)(2,1)S(1)}, u32[]{:S(2)}, u32[]{:S(2)}) collective-permute-start(bf16[32,1024]{1,0:T(8,128)(2,1)S(1)} %get-tuple-element.49), channel_id=1, source_target_pairs={{0,8},{8,0},{16,24},{24,16},{1,9},{9,1},{17,25},{25,17},{2,10},{10... | collective-permute-start | bytes 196616 | tf_op jit(solution)/shard_map/ppermute | solution.py:275
  11.1 5.3 %collective-permute-start.2 = (bf16[32,1024]{1,0:T(8,128)(2,1)S(1)}, bf16[32,1024]{1,0:T(8,128)(2,1)S(1)}, u32[]{:S(2)}, u32[]{:S(2)}) collective-permute-start(bf16[32,1024]{1,0:T(8,128)(2,1)S(1)} %get-tuple-element.50), channel_id=1, source_target_pairs={{0,16},{8,24},{16,0},{24,8},{1,17},{9,25},{17,1},{25,9},{2,18},{10... | collective-permute-start | bytes 196616 | tf_op jit(solution)/shard_map/ppermute | solution.py:275
  12.7 5.2 %collective-permute-start.3 = (bf16[32,1024]{1,0:T(8,128)(2,1)S(1)}, bf16[32,1024]{1,0:T(8,128)(2,1)S(1)}, u32[]{:S(2)}, u32[]{:S(2)}) collective-permute-start(bf16[32,1024]{1,0:T(8,128)(2,1)S(1)} %get-tuple-element.51), channel_id=1, source_target_pairs={{0,24},{8,16},{16,8},{24,0},{1,25},{9,17},{17,9},{25,1},{2,26},{10... | collective-permute-start | bytes 196616 | tf_op jit(solution)/shard_map/ppermute | solution.py:275
  13.6 6.0 %collective-permute-start.8 = (bf16[16,4096]{1,0:T(8,128)(2,1)S(1)}, bf16[16,4096]{1,0:T(8,128)(2,1)S(1)}, u32[]{:S(2)}, u32[]{:S(2)}) collective-permute-start(bf16[16,4096]{1,0:T(8,128)(2,1)S(1)} %slice_bitcast_fusion.1), channel_id=1, source_target_pairs={{0,2},{1,3},{2,6},{3,7},{6,4},{7,5},{4,0},{5,1},{8,10},{9,11},{10,... | collective-permute-start | bytes 393224 | tf_op jit(solution)/shard_map/ppermute | solution.py:269
  17.9 1.8 copy-start.7
  19.7 23.6 %collective-permute-start.4 = (bf16[1024,512]{1,0:T(8,128)(2,1)}, bf16[1024,512]{1,0:T(8,128)(2,1)S(1)}, u32[]{:S(2)}, u32[]{:S(2)}) collective-permute-start(bf16[1024,512]{1,0:T(8,128)(2,1)} %refs_0_.5), channel_id=1, source_target_pairs={{0,8},{8,0},{16,24},{24,16},{1,9},{9,1},{17,25},{25,17},{2,10},{10... | collective-permute-start | bytes 3145736 | tf_op jit(solution)/shard_map/ppermute | solution.py:275
  21.6 23.2 %collective-permute-start.5 = (bf16[1024,512]{1,0:T(8,128)(2,1)}, bf16[1024,512]{1,0:T(8,128)(2,1)S(1)}, u32[]{:S(2)}, u32[]{:S(2)}) collective-permute-start(bf16[1024,512]{1,0:T(8,128)(2,1)} %refs_0_.5), channel_id=1, source_target_pairs={{0,16},{8,24},{16,0},{24,8},{1,17},{9,25},{17,1},{25,9},{2,18},{10... | collective-permute-start | bytes 3145736 | tf_op jit(solution)/shard_map/ppermute | solution.py:275
  24.3 41.5 %collective-permute-start.15 = (bf16[112,4096]{1,0:T(8,128)(2,1)S(1)}, bf16[112,4096]{1,0:T(8,128)(2,1)S(1)}, u32[]{:S(2)}, u32[]{:S(2)}) collective-permute-start(bf16[112,4096]{1,0:T(8,128)(2,1)S(1)} %slice_bitcast_fusion), channel_id=1, source_target_pairs={{0,2},{1,3},{2,6},{3,7},{6,4},{7,5},{4,0},{5,1},{8,10},{9,11},{10,... | collective-permute-start | bytes 2752520 | tf_op jit(solution)/shard_map/ppermute | solution.py:269
  44.8 24.5 %copy-start = (bf16[1024,512]{1,0:T(8,128)(2,1)}, bf16[1024,512]{1,0:T(8,128)(2,1)S(1)}, u32[]{:S(2)}) copy-start(bf16[1024,512]{1,0:T(8,128)(2,1)S(1)} %collective-permute-done.5.refs_2_) | copy-start | bytes 3145732
  44.8 24.5 %collective-permute-start.10 = (bf16[512,1024]{1,0:T(8,128)(2,1)}, bf16[512,1024]{1,0:T(8,128)(2,1)S(1)}, u32[]{:S(2)}, u32[]{:S(2)}) collective-permute-start(bf16[512,1024]{1,0:T(8,128)(2,1)} %refs_0_.7), channel_id=1, source_target_pairs={{0,16},{8,24},{16,0},{24,8},{1,17},{9,25},{17,1},{25,9},{2,18},{10... | collective-permute-start | bytes 3145736 | tf_op jit(solution)/shard_map/ppermute | solution.py:275
  47.0 29.4 %collective-permute-start.9 = (bf16[512,1024]{1,0:T(8,128)(2,1)}, bf16[512,1024]{1,0:T(8,128)(2,1)S(1)}, u32[]{:S(2)}, u32[]{:S(2)}) collective-permute-start(bf16[512,1024]{1,0:T(8,128)(2,1)} %refs_0_.7), channel_id=1, source_target_pairs={{0,8},{8,0},{16,24},{24,16},{1,9},{9,1},{17,25},{25,17},{2,10},{10... | collective-permute-start | bytes 3145736 | tf_op jit(solution)/shard_map/ppermute | solution.py:275
  66.8 19.6 %collective-permute-start.16 = (bf16[128,4096]{1,0:T(8,128)(2,1)}, bf16[128,4096]{1,0:T(8,128)(2,1)}, u32[]{:S(2)}, u32[]{:S(2)}) collective-permute-start(bf16[128,4096]{1,0:T(8,128)(2,1)} %constant_dynamic-update-slice_fusion.5.mine), channel_id=1, source_target_pairs={{0,2},{1,3},{2,6},{3,7},{6,4},{7,5},{4,0},{5,1},{8,10},{9,11},{10,... | collective-permute-start | bytes 3145736 | tf_op jit(solution)/shard_map/ppermute | solution.py:269
  66.8 22.5 %collective-permute-start.20 = (bf16[128,4096]{1,0:T(8,128)(2,1)}, bf16[128,4096]{1,0:T(8,128)(2,1)}, u32[]{:S(2)}, u32[]{:S(2)}) collective-permute-start(bf16[128,4096]{1,0:T(8,128)(2,1)} %constant_dynamic-update-slice_fusion.5.mine), channel_id=1, source_target_pairs={{0,1},{1,0},{2,3},{3,2},{4,5},{5,4},{6,7},{7,6},{8,9},{9,8},{10,11... | collective-permute-start | bytes 3145736 | tf_op jit(solution)/shard_map/ppermute | solution.py:272
  67.7 14.7 %collective-permute-start.6 = (bf16[512,512]{1,0:T(8,128)(2,1)}, bf16[512,512]{1,0:T(8,128)(2,1)}, u32[]{:S(2)}, u32[]{:S(2)}) collective-permute-start(bf16[512,512]{1,0:T(8,128)(2,1)} %slice.32), channel_id=1, source_target_pairs={{0,16},{8,24},{16,0},{24,8},{1,17},{9,25},{17,1},{25,9},{2,18},{10... | collective-permute-start | bytes 1572872 | tf_op jit(solution)/shard_map/ppermute | solution.py:275
  69.3 15.1 %collective-permute-start.7 = (bf16[512,512]{1,0:T(8,128)(2,1)}, bf16[512,512]{1,0:T(8,128)(2,1)}, u32[]{:S(2)}, u32[]{:S(2)}) collective-permute-start(bf16[512,512]{1,0:T(8,128)(2,1)} %slice.33), channel_id=1, source_target_pairs={{0,8},{8,0},{16,24},{24,16},{1,9},{9,1},{17,25},{25,17},{2,10},{10... | collective-permute-start | bytes 1572872 | tf_op jit(solution)/shard_map/ppermute | solution.py:275
  70.0 19.2 %copy-start.1 = (bf16[1024,512]{1,0:T(8,128)(2,1)S(1)}, bf16[1024,512]{1,0:T(8,128)(2,1)}, u32[]{:S(2)}) copy-start(bf16[1024,512]{1,0:T(8,128)(2,1)} %copy-done) | copy-start | bytes 3145732
  70.0 19.2 %copy-start.2 = (bf16[1024,512]{1,0:T(8,128)(2,1)S(1)}, bf16[1024,512]{1,0:T(8,128)(2,1)}, u32[]{:S(2)}) copy-start(bf16[1024,512]{1,0:T(8,128)(2,1)} %refs_0_.5) | copy-start | bytes 3145732
  76.3 19.2 %collective-permute-start.11 = (bf16[256,1024]{1,0:T(8,128)(2,1)}, bf16[256,1024]{1,0:T(8,128)(2,1)S(1)}, u32[]{:S(2)}, u32[]{:S(2)}) collective-permute-start(bf16[256,1024]{1,0:T(8,128)(2,1)} %get-tuple-element.65), channel_id=1, source_target_pairs={{0,8},{8,0},{16,24},{24,16},{1,9},{9,1},{17,25},{25,17},{2,10},{10... | collective-permute-start | bytes 1572872 | tf_op jit(solution)/shard_map/ppermute | solution.py:275
  82.3 25.4 %collective-permute-start.12 = (bf16[256,1024]{1,0:T(8,128)(2,1)}, bf16[256,1024]{1,0:T(8,128)(2,1)S(1)}, u32[]{:S(2)}, u32[]{:S(2)}) collective-permute-start(bf16[256,1024]{1,0:T(8,128)(2,1)} %get-tuple-element.66), channel_id=1, source_target_pairs={{0,16},{8,24},{16,0},{24,8},{1,17},{9,25},{17,1},{25,9},{2,18},{10... | collective-permute-start | bytes 1572872 | tf_op jit(solution)/shard_map/ppermute | solution.py:275
  84.4 24.1 %collective-permute-start.13 = (bf16[256,1024]{1,0:T(8,128)(2,1)}, bf16[256,1024]{1,0:T(8,128)(2,1)S(1)}, u32[]{:S(2)}, u32[]{:S(2)}) collective-permute-start(bf16[256,1024]{1,0:T(8,128)(2,1)} %get-tuple-element.67), channel_id=1, source_target_pairs={{0,24},{8,16},{16,8},{24,0},{1,25},{9,17},{17,9},{25,1},{2,26},{10... | collective-permute-start | bytes 1572872 | tf_op jit(solution)/shard_map/ppermute | solution.py:275
  86.4 33.0 %collective-permute-start.17 = (bf16[128,4096]{1,0:T(8,128)(2,1)}, bf16[128,4096]{1,0:T(8,128)(2,1)S(1)}, u32[]{:S(2)}, u32[]{:S(2)}) collective-permute-start(bf16[128,4096]{1,0:T(8,128)(2,1)} %collective-permute-done.16.mine), channel_id=1, source_target_pairs={{0,2},{1,3},{2,6},{3,7},{6,4},{7,5},{4,0},{5,1},{8,10},{9,11},{10,... | collective-permute-start | bytes 3145736 | tf_op jit(solution)/shard_map/ppermute | solution.py:269
  89.3 33.8 %collective-permute-start.24 = (bf16[128,4096]{1,0:T(8,128)(2,1)}, bf16[128,4096]{1,0:T(8,128)(2,1)S(1)}, u32[]{:S(2)}, u32[]{:S(2)}) collective-permute-start(bf16[128,4096]{1,0:T(8,128)(2,1)} %collective-permute-done.16.mine), channel_id=1, source_target_pairs={{0,1},{1,0},{2,3},{3,2},{4,5},{5,4},{6,7},{7,6},{8,9},{9,8},{10,11... | collective-permute-start | bytes 3145736 | tf_op jit(solution)/shard_map/ppermute | solution.py:272
  92.8 15.7 %copy-start.6 = (f32[256,1024]{1,0:T(8,128)S(1)}, f32[256,1024]{1,0:T(8,128)}, u32[]{:S(2)}) copy-start(f32[256,1024]{1,0:T(8,128)} %get-tuple-element.64) | copy-start | bytes 3145732
  92.9 16.0 %copy-start.5 = (f32[8,256]{1,0:T(8,128)S(1)}, f32[8,256]{1,0:T(8,128)}, u32[]{:S(2)}) copy-start(f32[8,256]{1,0:T(8,128)} %get-tuple-element.58.open_ref) | copy-start | bytes 24580
  95.5 23.1 %collective-permute-start.21 = (bf16[256,1024]{1,0:T(8,128)(2,1)S(1)}, bf16[256,1024]{1,0:T(8,128)(2,1)S(1)}, u32[]{:S(2)}, u32[]{:S(2)}) collective-permute-start(bf16[256,1024]{1,0:T(8,128)(2,1)S(1)} %slice.30), channel_id=1, source_target_pairs={{0,16},{8,24},{16,0},{24,8},{1,17},{9,25},{17,1},{25,9},{2,18},{10... | collective-permute-start | bytes 1572872 | tf_op jit(solution)/shard_map/ppermute | solution.py:275
  107.7 10.8 %collective-permute-start.22 = (bf16[256,1024]{1,0:T(8,128)(2,1)S(1)}, bf16[256,1024]{1,0:T(8,128)(2,1)S(1)}, u32[]{:S(2)}, u32[]{:S(2)}) collective-permute-start(bf16[256,1024]{1,0:T(8,128)(2,1)S(1)} %slice.31), channel_id=1, source_target_pairs={{0,8},{8,0},{16,24},{24,16},{1,9},{9,1},{17,25},{25,17},{2,10},{10... | collective-permute-start | bytes 1572872 | tf_op jit(solution)/shard_map/ppermute | solution.py:275
  113.0 6.8 %collective-permute-start.25 = (bf16[128,2048]{1,0:T(8,128)(2,1)S(1)}, bf16[128,2048]{1,0:T(8,128)(2,1)S(1)}, u32[]{:S(2)}, u32[]{:S(2)}) collective-permute-start(bf16[128,2048]{1,0:T(8,128)(2,1)S(1)} %get-tuple-element.79), channel_id=1, source_target_pairs={{0,1},{1,0},{2,3},{3,2},{4,5},{5,4},{6,7},{7,6},{8,9},{9,8},{10,11... | collective-permute-start | bytes 1572872 | tf_op jit(solution)/shard_map/ppermute | solution.py:272
  119.3 7.0 %collective-permute-start.23 = (bf16[128,2048]{1,0:T(8,128)(2,1)S(1)}, bf16[128,2048]{1,0:T(8,128)(2,1)S(1)}, u32[]{:S(2)}, u32[]{:S(2)}) collective-permute-start(bf16[128,2048]{1,0:T(8,128)(2,1)S(1)} %get-tuple-element.76), channel_id=1, source_target_pairs={{0,1},{1,0},{2,3},{3,2},{4,5},{5,4},{6,7},{7,6},{8,9},{9,8},{10,11... | collective-permute-start | bytes 1572872 | tf_op jit(solution)/shard_map/ppermute | solution.py:272
  119.4 19.7 %collective-permute-start.18 = (bf16[128,4096]{1,0:T(8,128)(2,1)S(1)}, bf16[128,4096]{1,0:T(8,128)(2,1)S(1)}, u32[]{:S(2)}, u32[]{:S(2)}) collective-permute-start(bf16[128,4096]{1,0:T(8,128)(2,1)S(1)} %collective-permute-done.17.mine), channel_id=1, source_target_pairs={{0,1},{1,0},{2,3},{3,2},{4,5},{5,4},{6,7},{7,6},{8,9},{9,8},{10,11... | collective-permute-start | bytes 3145736 | tf_op jit(solution)/shard_map/ppermute | solution.py:272
  120.0 15.7 %collective-permute-start.26 = (bf16[128,2048]{1,0:T(8,128)(2,1)S(1)}, bf16[128,2048]{1,0:T(8,128)(2,1)S(1)}, u32[]{:S(2)}, u32[]{:S(2)}) collective-permute-start(bf16[128,2048]{1,0:T(8,128)(2,1)S(1)} %add_convert_fusion.4), channel_id=1, source_target_pairs={{0,2},{1,3},{2,6},{3,7},{6,4},{7,5},{4,0},{5,1},{8,10},{9,11},{10,... | collective-permute-start | bytes 1572872 | tf_op jit(solution)/shard_map/ppermute | solution.py:269
  126.3 10.3 %copy-start.3 = (bf16[1,1,128,4096]{3,2,1,0:T(8,128)(2,1)S(1)}, bf16[1,1,128,4096]{3,2,1,0:T(8,128)(2,1)}, u32[]{:S(2)}) copy-start(bf16[1,1,128,4096]{3,2,1,0:T(8,128)(2,1)} %param.8) | copy-start | bytes 3145732
  128.7 18.8 %collective-permute-start.33 = (bf16[128,2048]{1,0:T(8,128)(2,1)S(1)}, bf16[128,2048]{1,0:T(8,128)(2,1)S(1)}, u32[]{:S(2)}, u32[]{:S(2)}) collective-permute-start(bf16[128,2048]{1,0:T(8,128)(2,1)S(1)} %add_convert_fusion.5), channel_id=1, source_target_pairs={{0,2},{1,3},{2,6},{3,7},{6,4},{7,5},{4,0},{5,1},{8,10},{9,11},{10,... | collective-permute-start | bytes 1572872 | tf_op jit(solution)/shard_map/ppermute | solution.py:269
  136.5 11.1 %collective-permute-start.32 = (bf16[128,2048]{1,0:T(8,128)(2,1)S(1)}, bf16[128,2048]{1,0:T(8,128)(2,1)S(1)}, u32[]{:S(2)}, u32[]{:S(2)}) collective-permute-start(bf16[128,2048]{1,0:T(8,128)(2,1)S(1)} %get-tuple-element.89), channel_id=1, source_target_pairs={{0,1},{1,0},{2,3},{3,2},{4,5},{5,4},{6,7},{7,6},{8,9},{9,8},{10,11... | collective-permute-start | bytes 1572872 | tf_op jit(solution)/shard_map/ppermute | solution.py:272
  136.5 14.6 %collective-permute-start = (bf16[128,4096]{1,0:T(8,128)(2,1)S(1)}, bf16[128,4096]{1,0:T(8,128)(2,1)S(1)}, u32[]{:S(2)}, u32[]{:S(2)}) collective-permute-start(bf16[128,4096]{1,0:T(8,128)(2,1)S(1)} %bitcast.15), channel_id=1, source_target_pairs={{0,1},{1,0},{2,3},{3,2},{4,5},{5,4},{6,7},{7,6},{8,9},{9,8},{10,11... | collective-permute-start | bytes 3145736 | tf_op jit(solution)/shard_map/ppermute | solution.py:272
  139.0 11.0 %collective-permute-start.27 = (bf16[128,2048]{1,0:T(8,128)(2,1)S(1)}, bf16[128,2048]{1,0:T(8,128)(2,1)S(1)}, u32[]{:S(2)}, u32[]{:S(2)}) collective-permute-start(bf16[128,2048]{1,0:T(8,128)(2,1)S(1)} %get-tuple-element.82), channel_id=1, source_target_pairs={{0,1},{1,0},{2,3},{3,2},{4,5},{5,4},{6,7},{7,6},{8,9},{9,8},{10,11... | collective-permute-start | bytes 1572872 | tf_op jit(solution)/shard_map/ppermute | solution.py:272
  146.9 12.1 %collective-permute-start.31 = (bf16[128,2048]{1,0:T(8,128)(2,1)S(1)}, bf16[128,2048]{1,0:T(8,128)(2,1)S(1)}, u32[]{:S(2)}, u32[]{:S(2)}) collective-permute-start(bf16[128,2048]{1,0:T(8,128)(2,1)S(1)} %get-tuple-element.87), channel_id=1, source_target_pairs={{0,1},{1,0},{2,3},{3,2},{4,5},{5,4},{6,7},{7,6},{8,9},{9,8},{10,11... | collective-permute-start | bytes 1572872 | tf_op jit(solution)/shard_map/ppermute | solution.py:272
  147.4 17.5 %collective-permute-start.19 = (bf16[128,2048]{1,0:T(8,128)(2,1)S(1)}, bf16[128,2048]{1,0:T(8,128)(2,1)S(1)}, u32[]{:S(2)}, u32[]{:S(2)}) collective-permute-start(bf16[128,2048]{1,0:T(8,128)(2,1)S(1)} %get-tuple-element.73), channel_id=1, source_target_pairs={{0,1},{1,0},{2,3},{3,2},{4,5},{5,4},{6,7},{7,6},{8,9},{9,8},{10,11... | collective-permute-start | bytes 1572872 | tf_op jit(solution)/shard_map/ppermute | solution.py:272
  147.8 15.7 %collective-permute-start.34 = (bf16[128,2048]{1,0:T(8,128)(2,1)S(1)}, bf16[128,2048]{1,0:T(8,128)(2,1)S(1)}, u32[]{:S(2)}, u32[]{:S(2)}) collective-permute-start(bf16[128,2048]{1,0:T(8,128)(2,1)S(1)} %add_convert_fusion.1), channel_id=1, source_target_pairs={{0,2},{1,3},{2,6},{3,7},{6,4},{7,5},{4,0},{5,1},{8,10},{9,11},{10,... | collective-permute-start | bytes 1572872 | tf_op jit(solution)/shard_map/ppermute | solution.py:269
  150.2 24.5 %collective-permute-start.28 = (bf16[128,2048]{1,0:T(8,128)(2,1)S(1)}, bf16[128,2048]{1,0:T(8,128)(2,1)S(1)}, u32[]{:S(2)}, u32[]{:S(2)}) collective-permute-start(bf16[128,2048]{1,0:T(8,128)(2,1)S(1)} %add_convert_fusion.3), channel_id=1, source_target_pairs={{0,2},{1,3},{2,6},{3,7},{6,4},{7,5},{4,0},{5,1},{8,10},{9,11},{10,... | collective-permute-start | bytes 1572872 | tf_op jit(solution)/shard_map/ppermute | solution.py:269
  158.9 17.9 %collective-permute-start.30 = (bf16[128,2048]{1,0:T(8,128)(2,1)S(1)}, bf16[128,2048]{1,0:T(8,128)(2,1)S(1)}, u32[]{:S(2)}, u32[]{:S(2)}) collective-permute-start(bf16[128,2048]{1,0:T(8,128)(2,1)S(1)} %get-tuple-element.85), channel_id=1, source_target_pairs={{0,1},{1,0},{2,3},{3,2},{4,5},{5,4},{6,7},{7,6},{8,9},{9,8},{10,11... | collective-permute-start | bytes 1572872 | tf_op jit(solution)/shard_map/ppermute | solution.py:272
  159.0 17.8 %collective-permute-start.14 = (bf16[128,2048]{1,0:T(8,128)(2,1)S(1)}, bf16[128,2048]{1,0:T(8,128)(2,1)S(1)}, u32[]{:S(2)}, u32[]{:S(2)}) collective-permute-start(bf16[128,2048]{1,0:T(8,128)(2,1)S(1)} %get-tuple-element.70), channel_id=1, source_target_pairs={{0,1},{1,0},{2,3},{3,2},{4,5},{5,4},{6,7},{7,6},{8,9},{9,8},{10,11... | collective-permute-start | bytes 1572872 | tf_op jit(solution)/shard_map/ppermute | solution.py:272
  163.7 22.2 %collective-permute-start.35 = (bf16[128,2048]{1,0:T(8,128)(2,1)S(1)}, bf16[128,2048]{1,0:T(8,128)(2,1)S(1)}, u32[]{:S(2)}, u32[]{:S(2)}) collective-permute-start(bf16[128,2048]{1,0:T(8,128)(2,1)S(1)} %add_convert_fusion), channel_id=1, source_target_pairs={{0,2},{1,3},{2,6},{3,7},{6,4},{7,5},{4,0},{5,1},{8,10},{9,11},{10,... | collective-permute-start | bytes 1572872 | tf_op jit(solution)/shard_map/ppermute | solution.py:269
  174.9 21.8 %collective-permute-start.29 = (bf16[128,2048]{1,0:T(8,128)(2,1)S(1)}, bf16[128,2048]{1,0:T(8,128)(2,1)S(1)}, u32[]{:S(2)}, u32[]{:S(2)}) collective-permute-start(bf16[128,2048]{1,0:T(8,128)(2,1)S(1)} %add_convert_fusion.2), channel_id=1, source_target_pairs={{0,2},{1,3},{2,6},{3,7},{6,4},{7,5},{4,0},{5,1},{8,10},{9,11},{10,... | collective-permute-start | bytes 1572872 | tf_op jit(solution)/shard_map/ppermute | solution.py:269
Sparse Core Ops, SparseCore 0:
  19.8 45.7 all-gather.2

commit v2 on v1

--- a/solution.py
+++ b/solution.py
@@ -341,8 +341,8 @@
             if index:
                 total = total + passed[chunk].astype(f32)
             totals.append(total.astype(bf16))
-        if not index:
-            totals[1], queries[1] = barrier((totals[1], queries[1]))
+            if not index and not chunk:
+                context, totals[0] = barrier((context, totals[0]))
         if step:
             passed = [to_next(total) for total in totals]
     return finish(ids, counts, last, parts, width).reshape(cand_states.shape)

time: 206 us -> 206 us (level)
    ppermute x10, waiting for transfers between devices: 60.8 us -> 56.1 us  [to_next(): return lax.ppermute(value, 'cand', along)]
    ppermute x14, waiting for transfers between devices: 46 us -> 49.8 us  [flip(): return lax.ppermute(value, 'prod', [(q, q ^ r) for q in range(parts)])]
  transfers between devices with their start and end apart: 37 -> 37, of which waited for: 16 -> 17; matrix products, arithmetic and copies ran while one was open for 4% -> 4% of each run, Pallas kernels for 19% -> 19%
where the time goes in v2:
time: 206 us
  waiting for transfers between devices  106 us (51%)
  Pallas kernels  41 us (20%)
  starting transfers between devices  35.6 us (17%)
  between operations  14.4 us (7%)
  local copies, waits for them, and re-layouts  6.75 us (3%)
  other arithmetic  2.3 us (1%)
    ppermute x10, waiting for transfers between devices, to_next(): return lax.ppermute(value, 'cand', along)  56.1 us
    ppermute x14, waiting for transfers between devices, flip(): return lax.ppermute(value, 'prod', [(q, q ^ r) for q in range(parts)])  49.8 us
    ppermute x14, starting transfers between devices, flip(): return lax.ppermute(value, 'prod', [(q, q ^ r) for q in range(parts)])  16.6 us
    ppermute x10, starting transfers between devices, to_next(): return lax.ppermute(value, 'cand', along)  16.4 us
    pallas_call x4, Pallas kernels, query(): pl.pallas_call(functools.partial(query_kernel, len(weights), parts), out_...  12.5 us
    pallas_call x8, Pallas kernels, project(): pl.pallas_call(functools.partial(project_kernel, pieces), out_shape=[shap...  10.6 us
    pallas_call x4, Pallas kernels, attend(): pl.pallas_call(functools.partial(attend_kernel, order, step), out_shape=j...  9 us
    pallas_call x1, Pallas kernels, key_value(): pl.pallas_call(functools.partial(key_value_kernel, parts, rows, tiles), o...  6.28 us
  transfers between devices with their start and end apart: 37, of which 17 were waited for; matrix products, arithmetic and copies ran while one was open for 4% of the time, Pallas kernels for 19%

profile of v2, /device:TPU:0, one launch (start us, length us, event | category | flops | bytes accessed | tf_op | source)
XLA Modules:
  0.0 205.9 jit_solution(13319726916955088945)
XLA Ops:
  6.6 0.9 copy-done.4
  7.6 0.6 columns.1
  8.1 3.0 %collective-permute-start.1 = (bf16[32,1024]{1,0:T(8,128)(2,1)S(1)}, bf16[32,1024]{1,0:T(8,128)(2,1)S(1)}, u32[]{:S(2)}, u32[]{:S(2)}) collective-permute-start(bf16[32,1024]{1,0:T(8,128)(2,1)S(1)} %get-tuple-element.49), channel_id=1, source_target_pairs={{0,8},{8,0},{16,24},{24,16},{1,9},{9,1},{17,25},{25,17},{2,10},{10... | collective-permute-start | bytes 196616 | tf_op jit(solution)/shard_map/ppermute | solution.py:275
  11.1 1.5 collective-permute-start.2
  12.7 0.9 slice_bitcast_fusion.1
  13.6 2.1 %collective-permute-start.8 = (bf16[16,4096]{1,0:T(8,128)(2,1)S(1)}, bf16[16,4096]{1,0:T(8,128)(2,1)S(1)}, u32[]{:S(2)}, u32[]{:S(2)}) collective-permute-start(bf16[16,4096]{1,0:T(8,128)(2,1)S(1)} %slice_bitcast_fusion.1), channel_id=1, source_target_pairs={{0,2},{1,3},{2,6},{3,7},{6,4},{7,5},{4,0},{5,1},{8,10},{9,11},{10,... | collective-permute-start | bytes 393224 | tf_op jit(solution)/shard_map/ppermute | solution.py:269
  15.7 0.7 convert_bitcast_fusion
  16.4 1.4 collective-permute-done.3
  17.9 1.7 collective-permute-done.8
  19.7 1.9 collective-permute-start.4
  21.6 1.5 collective-permute-start.5
  23.1 1.2 slice_bitcast_fusion
  24.3 0.9 collective-permute-start.15
  25.2 18.1 %collective-permute-done.4.refs_1_ = bf16[1024,512]{1,0:T(8,128)(2,1)S(1)} collective-permute-done((bf16[1024,512]{1,0:T(8,128)(2,1)}, bf16[1024,512]{1,0:T(8,128)(2,1)S(1)}, u32[]{:S(2)}, u32[]{:S(2)}) %collective-permute-start.4) | collective-permute-done | bytes 1048608 | tf_op jit(solution)/shard_map/ppermute | solution.py:275
  43.3 1.1 collective-permute-done.5.refs_2_
  44.4 0.7 collective-permute-start.9
  45.1 0.7 constant_dynamic-update-slice_fusion.6
  45.7 1.4 collective-permute-start.10
  47.1 18.7 %collective-permute-done.15 = bf16[112,4096]{1,0:T(8,128)(2,1)S(1)} collective-permute-done((bf16[112,4096]{1,0:T(8,128)(2,1)S(1)}, bf16[112,4096]{1,0:T(8,128)(2,1)S(1)}, u32[]{:S(2)}, u32[]{:S(2)}) %collective-permute-start.15) | collective-permute-done | bytes 917536 | tf_op jit(solution)/shard_map/ppermute | solution.py:269
  65.8 1.0 constant_dynamic-update-slice_fusion.5.mine
  66.8 0.9 slice.32
  67.7 0.7 collective-permute-start.6
  68.4 0.9 slice.33
  69.3 0.8 collective-permute-start.7
  70.1 6.3 %key_value.1 = (f32[8,256]{1,0:T(8,128)}, f32[256,1024]{1,0:T(8,128)}, bf16[256,1024]{1,0:T(8,128)(2,1)}, bf16[256,1024]{1,0:T(8,128)(2,1)}, bf16[256,1024]{1,0:T(8,128)(2,1)}) custom-call(bf16[8,144,1024]{2,1,0:T(8,128)(2,1)} %bitcast.19, bf16[1024,512]{1,0:T(8,128)(2,1)} %w_key.1, bf16[1024,512]{1,0:T(8,128)(2,1)} %w_value.1), custom_call_target="tpu_custom_call" | custom-call | flops 3000000000 | bytes 1 | tf_op jit(solution)/shard_map/key_value/pallas_call | solution.py:76
  76.3 2.0 collective-permute-start.13
  78.3 4.0 %collective-permute-done.6.refs_3_ = bf16[512,512]{1,0:T(8,128)(2,1)} collective-permute-done((bf16[512,512]{1,0:T(8,128)(2,1)}, bf16[512,512]{1,0:T(8,128)(2,1)}, u32[]{:S(2)}, u32[]{:S(2)}) %collective-permute-start.6) | collective-permute-done | bytes 524320 | tf_op jit(solution)/shard_map/ppermute | solution.py:275
  82.3 0.7 collective-permute-start.12
  83.1 1.3 collective-permute-done.7.refs_4_
  84.4 0.8 collective-permute-start.11
  85.1 1.3 collective-permute-done.16.mine
  86.4 2.1 %collective-permute-start.17 = (bf16[128,4096]{1,0:T(8,128)(2,1)}, bf16[128,4096]{1,0:T(8,128)(2,1)S(1)}, u32[]{:S(2)}, u32[]{:S(2)}) collective-permute-start(bf16[128,4096]{1,0:T(8,128)(2,1)} %collective-permute-done.16.mine), channel_id=1, source_target_pairs={{0,2},{1,3},{2,6},{3,7},{6,4},{7,5},{4,0},{5,1},{8,10},{9,11},{10,... | collective-permute-start | bytes 3145736 | tf_op jit(solution)/shard_map/ppermute | solution.py:269
  88.5 3.5 %query.7.query_ref = bf16[256,512]{1,0:T(8,128)(2,1)S(1)} custom-call(s32[2]{0:T(128)S(1)} %pad_add_fusion.ids, bf16[128,4096]{1,0:T(8,128)(2,1)} %constant_dynamic-update-slice_fusion.5.mine, bf16[128,4096]{1,0:T(8,128)(2,1)} %collective-permute-done.21.sib, bf16[1024,512]{1,0:T(8,128)(2,1)S(1)} %copy-done.2, ...), custom_call_target="tpu_custom_call" | custom-call | flops 1 | bytes 1 | tf_op jit(solution)/shard_map/query/pallas_call | solution.py:119
  92.1 4.2 %collective-permute-done.13 = bf16[256,1024]{1,0:T(8,128)(2,1)S(1)} collective-permute-done((bf16[256,1024]{1,0:T(8,128)(2,1)}, bf16[256,1024]{1,0:T(8,128)(2,1)S(1)}, u32[]{:S(2)}, u32[]{:S(2)}) %collective-permute-start.13) | collective-permute-done | bytes 524320 | tf_op jit(solution)/shard_map/ppermute | solution.py:275
  96.3 10.4 %collective-permute-done.12 = bf16[256,1024]{1,0:T(8,128)(2,1)S(1)} collective-permute-done((bf16[256,1024]{1,0:T(8,128)(2,1)}, bf16[256,1024]{1,0:T(8,128)(2,1)S(1)}, u32[]{:S(2)}, u32[]{:S(2)}) %collective-permute-start.12) | collective-permute-done | bytes 524320 | tf_op jit(solution)/shard_map/ppermute | solution.py:275
  107.0 2.3 %attend.7.context_ref = bf16[256,512]{1,0:T(8,128)(2,1)S(1)} custom-call(s32[2]{0:T(128)S(1)} %pad_add_fusion.ids, bf16[256,512]{1,0:T(8,128)(2,1)S(1)} %query.7.query_ref, f32[8,256]{1,0:T(8,128)S(1)} %copy-done.5, bf16[256,1024]{1,0:T(8,128)(2,1)S(1)} %add_convert_fusion.6.kv_ref), custom_call_target="tpu_custom_call" | custom-call | flops 1 | bytes 1 | tf_op jit(solution)/shard_map/attend/pallas_call | solution.py:179
  109.3 1.9 project.10
  111.9 0.8 collective-permute-start.27
  112.7 0.8 collective-permute-start.28
  113.7 3.4 %collective-permute-start.23 = (bf16[128,2048]{1,0:T(8,128)(2,1)S(1)}, bf16[128,2048]{1,0:T(8,128)(2,1)S(1)}, u32[]{:S(2)}, u32[]{:S(2)}) collective-permute-start(bf16[128,2048]{1,0:T(8,128)(2,1)S(1)} %add_convert_fusion.5), channel_id=1, source_target_pairs={{0,2},{1,3},{2,6},{3,7},{6,4},{7,5},{4,0},{5,1},{8,10},{9,11},{10,... | collective-permute-start | bytes 1572872 | tf_op jit(solution)/shard_map/ppermute | solution.py:269
  117.1 8.7 %collective-permute-done.27.refs_1_ = bf16[256,1024]{1,0:T(8,128)(2,1)S(1)} collective-permute-done((bf16[256,1024]{1,0:T(8,128)(2,1)S(1)}, bf16[256,1024]{1,0:T(8,128)(2,1)S(1)}, u32[]{:S(2)}, u32[]{:S(2)}) %collective-permute-start.27) | collective-permute-done | bytes 524320 | tf_op jit(solution)/shard_map/ppermute | solution.py:275
  126.4 0.7 project.15
  127.2 3.2 %query.6.query_ref = bf16[256,512]{1,0:T(8,128)(2,1)S(1)} custom-call(s32[2]{0:T(128)S(1)} %pad_add_fusion.ids, bf16[128,4096]{1,0:T(8,128)(2,1)} %collective-permute-done.16.mine, bf16[128,4096]{1,0:T(8,128)(2,1)S(1)} %collective-permute-done.20.sib, bf16[1024,512]{1,0:T(8,128)(2,1)S(1)} %copy-done.2, bf16[1024,512]{1,0:T(8,128)(2,1)S(1)} %collective-permute-done.4.refs_1_, ...), custom_call_target="tpu_custom_call" | custom-call | flops 1 | bytes 1 | tf_op jit(solution)/shard_map/query/pallas_call | solution.py:119
  130.4 2.3 %attend.6.context_ref = bf16[256,512]{1,0:T(8,128)(2,1)S(1)} custom-call(s32[2]{0:T(128)S(1)} %pad_add_fusion.ids, bf16[256,512]{1,0:T(8,128)(2,1)S(1)} %query.6.query_ref, f32[8,256]{1,0:T(8,128)S(1)} %copy-done.5, bf16[256,1024]{1,0:T(8,128)(2,1)S(1)} %add_convert_fusion.6.kv_ref), custom_call_target="tpu_custom_call" | custom-call | flops 1 | bytes 1 | tf_op jit(solution)/shard_map/attend/pallas_call | solution.py:179
  132.7 1.9 project.11
  135.4 3.6 %collective-permute-start.33 = (bf16[128,2048]{1,0:T(8,128)(2,1)S(1)}, bf16[128,2048]{1,0:T(8,128)(2,1)S(1)}, u32[]{:S(2)}, u32[]{:S(2)}) collective-permute-start(bf16[128,2048]{1,0:T(8,128)(2,1)S(1)} %add_convert_fusion.2), channel_id=1, source_target_pairs={{0,2},{1,3},{2,6},{3,7},{6,4},{7,5},{4,0},{5,1},{8,10},{9,11},{10,... | collective-permute-start | bytes 1572872 | tf_op jit(solution)/shard_map/ppermute | solution.py:269
  139.0 0.7 project.14
  140.0 2.9 %query.5.query_ref = bf16[256,512]{1,0:T(8,128)(2,1)S(1)} custom-call(s32[2]{0:T(128)S(1)} %pad_add_fusion.ids, bf16[128,4096]{1,0:T(8,128)(2,1)S(1)} %collective-permute-done.17.mine, bf16[128,4096]{1,0:T(8,128)(2,1)S(1)} %collective-permute-done.18.sib, bf16[1024,512]{1,0:T(8,128)(2,1)S(1)} %copy-done.2, ...), custom_call_target="tpu_custom_call" | custom-call | flops 1 | bytes 1 | tf_op jit(solution)/shard_map/query/pallas_call | solution.py:119
  142.9 2.2 %attend.5.context_ref = bf16[256,512]{1,0:T(8,128)(2,1)S(1)} custom-call(s32[2]{0:T(128)S(1)} %pad_add_fusion.ids, bf16[256,512]{1,0:T(8,128)(2,1)S(1)} %query.5.query_ref, f32[8,256]{1,0:T(8,128)S(1)} %copy-done.5, bf16[256,1024]{1,0:T(8,128)(2,1)S(1)} %add_convert_fusion.6.kv_ref), custom_call_target="tpu_custom_call" | custom-call | flops 1 | bytes 1 | tf_op jit(solution)/shard_map/attend/pallas_call | solution.py:179
  145.1 1.9 project.9
  147.5 0.7 project.13
  148.6 2.7 %collective-permute-done.33 = bf16[128,2048]{1,0:T(8,128)(2,1)S(1)} collective-permute-done((bf16[128,2048]{1,0:T(8,128)(2,1)S(1)}, bf16[128,2048]{1,0:T(8,128)(2,1)S(1)}, u32[]{:S(2)}, u32[]{:S(2)}) %collective-permute-start.33) | collective-permute-done | bytes 524320 | tf_op jit(solution)/shard_map/ppermute | solution.py:269
  151.5 2.5 %collective-permute-start.34 = (bf16[128,2048]{1,0:T(8,128)(2,1)S(1)}, bf16[128,2048]{1,0:T(8,128)(2,1)S(1)}, u32[]{:S(2)}, u32[]{:S(2)}) collective-permute-start(bf16[128,2048]{1,0:T(8,128)(2,1)S(1)} %add_convert_fusion.1), channel_id=1, source_target_pairs={{0,2},{1,3},{2,6},{3,7},{6,4},{7,5},{4,0},{5,1},{8,10},{9,11},{10,... | collective-permute-start | bytes 1572872 | tf_op jit(solution)/shard_map/ppermute | solution.py:269
  154.1 2.9 %query.4.query_ref = bf16[256,512]{1,0:T(8,128)(2,1)S(1)} custom-call(s32[2]{0:T(128)S(1)} %pad_add_fusion.ids, bf16[128,4096]{1,0:T(8,128)(2,1)S(1)} %bitcast.16, bf16[128,4096]{1,0:T(8,128)(2,1)S(1)} %collective-permute-done.sib, bf16[1024,512]{1,0:T(8,128)(2,1)S(1)} %copy-done.2, bf16[1024,512]{1,0:T(8,128)(2,1)S(1)} %collective-permute-done.4.refs_1_, ...), custom_call_target="tpu_custom_call" | custom-call | flops 1 | bytes 1 | tf_op jit(solution)/shard_map/query/pallas_call | solution.py:119
  157.0 2.2 %attend.4.context_ref = bf16[256,512]{1,0:T(8,128)(2,1)S(1)} custom-call(s32[2]{0:T(128)S(1)} %pad_add_fusion.ids, bf16[256,512]{1,0:T(8,128)(2,1)S(1)} %query.4.query_ref, f32[8,256]{1,0:T(8,128)S(1)} %copy-done.5, bf16[256,1024]{1,0:T(8,128)(2,1)S(1)} %add_convert_fusion.6.kv_ref), custom_call_target="tpu_custom_call" | custom-call | flops 1 | bytes 1 | tf_op jit(solution)/shard_map/attend/pallas_call | solution.py:179
  159.3 1.9 project.8
  161.5 0.7 project.12
  162.6 1.6 collective-permute-done.25
  164.5 0.8 collective-permute-start.26
  165.3 10.1 %collective-permute-done.34 = bf16[128,2048]{1,0:T(8,128)(2,1)S(1)} collective-permute-done((bf16[128,2048]{1,0:T(8,128)(2,1)S(1)}, bf16[128,2048]{1,0:T(8,128)(2,1)S(1)}, u32[]{:S(2)}, u32[]{:S(2)}) %collective-permute-start.34) | collective-permute-done | bytes 524320 | tf_op jit(solution)/shard_map/ppermute | solution.py:269
  175.7 0.8 collective-permute-start.35
  177.2 9.5 %collective-permute-done.26.refs_2_ = bf16[128,2048]{1,0:T(8,128)(2,1)S(1)} collective-permute-done((bf16[128,2048]{1,0:T(8,128)(2,1)S(1)}, bf16[128,2048]{1,0:T(8,128)(2,1)S(1)}, u32[]{:S(2)}, u32[]{:S(2)}) %collective-permute-start.26) | collective-permute-done | bytes 524320 | tf_op jit(solution)/shard_map/ppermute | solution.py:269
  186.7 10.4 %collective-permute-done.35.refs_5_ = bf16[128,2048]{1,0:T(8,128)(2,1)S(1)} collective-permute-done((bf16[128,2048]{1,0:T(8,128)(2,1)S(1)}, bf16[128,2048]{1,0:T(8,128)(2,1)S(1)}, u32[]{:S(2)}, u32[]{:S(2)}) %collective-permute-start.35) | collective-permute-done | bytes 524320 | tf_op jit(solution)/shard_map/ppermute | solution.py:269
  197.1 2.0 finish.1
  (70 shorter events, 5.2 us)
Async XLA Ops:
  6.5 63.5 %all-gather.3.cloned.1.call-start = ((), (), s32[]{:S(2)}) async-start(), calls=%async_computation | async-start | bytes 2654208 | tf_op jit(solution)/shard_map/all_gather | solution.py:307
  6.6 0.9 copy-start.4
  8.1 8.3 %collective-permute-start.1 = (bf16[32,1024]{1,0:T(8,128)(2,1)S(1)}, bf16[32,1024]{1,0:T(8,128)(2,1)S(1)}, u32[]{:S(2)}, u32[]{:S(2)}) collective-permute-start(bf16[32,1024]{1,0:T(8,128)(2,1)S(1)} %get-tuple-element.49), channel_id=1, source_target_pairs={{0,8},{8,0},{16,24},{24,16},{1,9},{9,1},{17,25},{25,17},{2,10},{10... | collective-permute-start | bytes 196616 | tf_op jit(solution)/shard_map/ppermute | solution.py:275
  11.1 5.3 %collective-permute-start.2 = (bf16[32,1024]{1,0:T(8,128)(2,1)S(1)}, bf16[32,1024]{1,0:T(8,128)(2,1)S(1)}, u32[]{:S(2)}, u32[]{:S(2)}) collective-permute-start(bf16[32,1024]{1,0:T(8,128)(2,1)S(1)} %get-tuple-element.50), channel_id=1, source_target_pairs={{0,16},{8,24},{16,0},{24,8},{1,17},{9,25},{17,1},{25,9},{2,18},{10... | collective-permute-start | bytes 196616 | tf_op jit(solution)/shard_map/ppermute | solution.py:275
  12.7 5.2 %collective-permute-start.3 = (bf16[32,1024]{1,0:T(8,128)(2,1)S(1)}, bf16[32,1024]{1,0:T(8,128)(2,1)S(1)}, u32[]{:S(2)}, u32[]{:S(2)}) collective-permute-start(bf16[32,1024]{1,0:T(8,128)(2,1)S(1)} %get-tuple-element.51), channel_id=1, source_target_pairs={{0,24},{8,16},{16,8},{24,0},{1,25},{9,17},{17,9},{25,1},{2,26},{10... | collective-permute-start | bytes 196616 | tf_op jit(solution)/shard_map/ppermute | solution.py:275
  13.6 6.0 %collective-permute-start.8 = (bf16[16,4096]{1,0:T(8,128)(2,1)S(1)}, bf16[16,4096]{1,0:T(8,128)(2,1)S(1)}, u32[]{:S(2)}, u32[]{:S(2)}) collective-permute-start(bf16[16,4096]{1,0:T(8,128)(2,1)S(1)} %slice_bitcast_fusion.1), channel_id=1, source_target_pairs={{0,2},{1,3},{2,6},{3,7},{6,4},{7,5},{4,0},{5,1},{8,10},{9,11},{10,... | collective-permute-start | bytes 393224 | tf_op jit(solution)/shard_map/ppermute | solution.py:269
  17.9 1.8 copy-start.7
  19.7 23.6 %collective-permute-start.4 = (bf16[1024,512]{1,0:T(8,128)(2,1)}, bf16[1024,512]{1,0:T(8,128)(2,1)S(1)}, u32[]{:S(2)}, u32[]{:S(2)}) collective-permute-start(bf16[1024,512]{1,0:T(8,128)(2,1)} %refs_0_.5), channel_id=1, source_target_pairs={{0,8},{8,0},{16,24},{24,16},{1,9},{9,1},{17,25},{25,17},{2,10},{10... | collective-permute-start | bytes 3145736 | tf_op jit(solution)/shard_map/ppermute | solution.py:275
  21.6 22.8 %collective-permute-start.5 = (bf16[1024,512]{1,0:T(8,128)(2,1)}, bf16[1024,512]{1,0:T(8,128)(2,1)S(1)}, u32[]{:S(2)}, u32[]{:S(2)}) collective-permute-start(bf16[1024,512]{1,0:T(8,128)(2,1)} %refs_0_.5), channel_id=1, source_target_pairs={{0,16},{8,24},{16,0},{24,8},{1,17},{9,25},{17,1},{25,9},{2,18},{10... | collective-permute-start | bytes 3145736 | tf_op jit(solution)/shard_map/ppermute | solution.py:275
  24.3 41.5 %collective-permute-start.15 = (bf16[112,4096]{1,0:T(8,128)(2,1)S(1)}, bf16[112,4096]{1,0:T(8,128)(2,1)S(1)}, u32[]{:S(2)}, u32[]{:S(2)}) collective-permute-start(bf16[112,4096]{1,0:T(8,128)(2,1)S(1)} %slice_bitcast_fusion), channel_id=1, source_target_pairs={{0,2},{1,3},{2,6},{3,7},{6,4},{7,5},{4,0},{5,1},{8,10},{9,11},{10,... | collective-permute-start | bytes 2752520 | tf_op jit(solution)/shard_map/ppermute | solution.py:269
  44.4 24.9 %copy-start = (bf16[1024,512]{1,0:T(8,128)(2,1)}, bf16[1024,512]{1,0:T(8,128)(2,1)S(1)}, u32[]{:S(2)}) copy-start(bf16[1024,512]{1,0:T(8,128)(2,1)S(1)} %collective-permute-done.5.refs_2_) | copy-start | bytes 3145732
  44.4 24.9 %collective-permute-start.9 = (bf16[512,1024]{1,0:T(8,128)(2,1)}, bf16[512,1024]{1,0:T(8,128)(2,1)S(1)}, u32[]{:S(2)}, u32[]{:S(2)}) collective-permute-start(bf16[512,1024]{1,0:T(8,128)(2,1)} %refs_0_.7), channel_id=1, source_target_pairs={{0,8},{8,0},{16,24},{24,16},{1,9},{9,1},{17,25},{25,17},{2,10},{10... | collective-permute-start | bytes 3145736 | tf_op jit(solution)/shard_map/ppermute | solution.py:275
  45.7 30.6 %collective-permute-start.10 = (bf16[512,1024]{1,0:T(8,128)(2,1)}, bf16[512,1024]{1,0:T(8,128)(2,1)S(1)}, u32[]{:S(2)}, u32[]{:S(2)}) collective-permute-start(bf16[512,1024]{1,0:T(8,128)(2,1)} %refs_0_.7), channel_id=1, source_target_pairs={{0,16},{8,24},{16,0},{24,8},{1,17},{9,25},{17,1},{25,9},{2,18},{10... | collective-permute-start | bytes 3145736 | tf_op jit(solution)/shard_map/ppermute | solution.py:275
  66.8 19.6 %collective-permute-start.16 = (bf16[128,4096]{1,0:T(8,128)(2,1)}, bf16[128,4096]{1,0:T(8,128)(2,1)}, u32[]{:S(2)}, u32[]{:S(2)}) collective-permute-start(bf16[128,4096]{1,0:T(8,128)(2,1)} %constant_dynamic-update-slice_fusion.5.mine), channel_id=1, source_target_pairs={{0,2},{1,3},{2,6},{3,7},{6,4},{7,5},{4,0},{5,1},{8,10},{9,11},{10,... | collective-permute-start | bytes 3145736 | tf_op jit(solution)/shard_map/ppermute | solution.py:269
  66.8 21.7 %collective-permute-start.21 = (bf16[128,4096]{1,0:T(8,128)(2,1)}, bf16[128,4096]{1,0:T(8,128)(2,1)}, u32[]{:S(2)}, u32[]{:S(2)}) collective-permute-start(bf16[128,4096]{1,0:T(8,128)(2,1)} %constant_dynamic-update-slice_fusion.5.mine), channel_id=1, source_target_pairs={{0,1},{1,0},{2,3},{3,2},{4,5},{5,4},{6,7},{7,6},{8,9},{9,8},{10,11... | collective-permute-start | bytes 3145736 | tf_op jit(solution)/shard_map/ppermute | solution.py:272
  67.7 14.7 %collective-permute-start.6 = (bf16[512,512]{1,0:T(8,128)(2,1)}, bf16[512,512]{1,0:T(8,128)(2,1)}, u32[]{:S(2)}, u32[]{:S(2)}) collective-permute-start(bf16[512,512]{1,0:T(8,128)(2,1)} %slice.32), channel_id=1, source_target_pairs={{0,16},{8,24},{16,0},{24,8},{1,17},{9,25},{17,1},{25,9},{2,18},{10... | collective-permute-start | bytes 1572872 | tf_op jit(solution)/shard_map/ppermute | solution.py:275
  69.3 15.1 %collective-permute-start.7 = (bf16[512,512]{1,0:T(8,128)(2,1)}, bf16[512,512]{1,0:T(8,128)(2,1)}, u32[]{:S(2)}, u32[]{:S(2)}) collective-permute-start(bf16[512,512]{1,0:T(8,128)(2,1)} %slice.33), channel_id=1, source_target_pairs={{0,8},{8,0},{16,24},{24,16},{1,9},{9,1},{17,25},{25,17},{2,10},{10... | collective-permute-start | bytes 1572872 | tf_op jit(solution)/shard_map/ppermute | solution.py:275
  70.0 18.5 %copy-start.1 = (bf16[1024,512]{1,0:T(8,128)(2,1)S(1)}, bf16[1024,512]{1,0:T(8,128)(2,1)}, u32[]{:S(2)}) copy-start(bf16[1024,512]{1,0:T(8,128)(2,1)} %copy-done) | copy-start | bytes 3145732
  70.0 18.5 %copy-start.2 = (bf16[1024,512]{1,0:T(8,128)(2,1)S(1)}, bf16[1024,512]{1,0:T(8,128)(2,1)}, u32[]{:S(2)}) copy-start(bf16[1024,512]{1,0:T(8,128)(2,1)} %refs_0_.5) | copy-start | bytes 3145732
  76.3 30.4 %copy-start.6 = (f32[256,1024]{1,0:T(8,128)S(1)}, f32[256,1024]{1,0:T(8,128)}, u32[]{:S(2)}) copy-start(f32[256,1024]{1,0:T(8,128)} %get-tuple-element.64) | copy-start | bytes 3145732
  76.3 19.9 %collective-permute-start.13 = (bf16[256,1024]{1,0:T(8,128)(2,1)}, bf16[256,1024]{1,0:T(8,128)(2,1)S(1)}, u32[]{:S(2)}, u32[]{:S(2)}) collective-permute-start(bf16[256,1024]{1,0:T(8,128)(2,1)} %get-tuple-element.67), channel_id=1, source_target_pairs={{0,24},{8,16},{16,8},{24,0},{1,25},{9,17},{17,9},{25,1},{2,26},{10... | collective-permute-start | bytes 1572872 | tf_op jit(solution)/shard_map/ppermute | solution.py:275
  82.3 24.4 %collective-permute-start.12 = (bf16[256,1024]{1,0:T(8,128)(2,1)}, bf16[256,1024]{1,0:T(8,128)(2,1)S(1)}, u32[]{:S(2)}, u32[]{:S(2)}) collective-permute-start(bf16[256,1024]{1,0:T(8,128)(2,1)} %get-tuple-element.66), channel_id=1, source_target_pairs={{0,16},{8,24},{16,0},{24,8},{1,17},{9,25},{17,1},{25,9},{2,18},{10... | collective-permute-start | bytes 1572872 | tf_op jit(solution)/shard_map/ppermute | solution.py:275
  84.4 22.3 %collective-permute-start.11 = (bf16[256,1024]{1,0:T(8,128)(2,1)}, bf16[256,1024]{1,0:T(8,128)(2,1)S(1)}, u32[]{:S(2)}, u32[]{:S(2)}) collective-permute-start(bf16[256,1024]{1,0:T(8,128)(2,1)} %get-tuple-element.65), channel_id=1, source_target_pairs={{0,8},{8,0},{16,24},{24,16},{1,9},{9,1},{17,25},{25,17},{2,10},{10... | collective-permute-start | bytes 1572872 | tf_op jit(solution)/shard_map/ppermute | solution.py:275
  86.4 27.1 %collective-permute-start.17 = (bf16[128,4096]{1,0:T(8,128)(2,1)}, bf16[128,4096]{1,0:T(8,128)(2,1)S(1)}, u32[]{:S(2)}, u32[]{:S(2)}) collective-permute-start(bf16[128,4096]{1,0:T(8,128)(2,1)} %collective-permute-done.16.mine), channel_id=1, source_target_pairs={{0,2},{1,3},{2,6},{3,7},{6,4},{7,5},{4,0},{5,1},{8,10},{9,11},{10,... | collective-permute-start | bytes 3145736 | tf_op jit(solution)/shard_map/ppermute | solution.py:269
  92.0 15.0 %copy-start.5 = (f32[8,256]{1,0:T(8,128)S(1)}, f32[8,256]{1,0:T(8,128)}, u32[]{:S(2)}) copy-start(f32[8,256]{1,0:T(8,128)} %get-tuple-element.58.open_ref) | copy-start | bytes 24580
  111.2 2.3 %collective-permute-start.22 = (bf16[128,2048]{1,0:T(8,128)(2,1)S(1)}, bf16[128,2048]{1,0:T(8,128)(2,1)S(1)}, u32[]{:S(2)}, u32[]{:S(2)}) collective-permute-start(bf16[128,2048]{1,0:T(8,128)(2,1)S(1)} %get-tuple-element.75), channel_id=1, source_target_pairs={{0,1},{1,0},{2,3},{3,2},{4,5},{5,4},{6,7},{7,6},{8,9},{9,8},{10,11... | collective-permute-start | bytes 1572872 | tf_op jit(solution)/shard_map/ppermute | solution.py:272
  111.3 15.9 %collective-permute-start.20 = (bf16[128,4096]{1,0:T(8,128)(2,1)}, bf16[128,4096]{1,0:T(8,128)(2,1)S(1)}, u32[]{:S(2)}, u32[]{:S(2)}) collective-permute-start(bf16[128,4096]{1,0:T(8,128)(2,1)} %collective-permute-done.16.mine), channel_id=1, source_target_pairs={{0,1},{1,0},{2,3},{3,2},{4,5},{5,4},{6,7},{7,6},{8,9},{9,8},{10,11... | collective-permute-start | bytes 3145736 | tf_op jit(solution)/shard_map/ppermute | solution.py:272
  111.9 14.0 %collective-permute-start.27 = (bf16[256,1024]{1,0:T(8,128)(2,1)S(1)}, bf16[256,1024]{1,0:T(8,128)(2,1)S(1)}, u32[]{:S(2)}, u32[]{:S(2)}) collective-permute-start(bf16[256,1024]{1,0:T(8,128)(2,1)S(1)} %slice.30), channel_id=1, source_target_pairs={{0,16},{8,24},{16,0},{24,8},{1,17},{9,25},{17,1},{25,9},{2,18},{10... | collective-permute-start | bytes 1572872 | tf_op jit(solution)/shard_map/ppermute | solution.py:275
  112.7 13.7 %collective-permute-start.28 = (bf16[256,1024]{1,0:T(8,128)(2,1)S(1)}, bf16[256,1024]{1,0:T(8,128)(2,1)S(1)}, u32[]{:S(2)}, u32[]{:S(2)}) collective-permute-start(bf16[256,1024]{1,0:T(8,128)(2,1)S(1)} %slice.31), channel_id=1, source_target_pairs={{0,8},{8,0},{16,24},{24,16},{1,9},{9,1},{17,25},{25,17},{2,10},{10... | collective-permute-start | bytes 1572872 | tf_op jit(solution)/shard_map/ppermute | solution.py:275
  113.5 26.5 %collective-permute-start.18 = (bf16[128,4096]{1,0:T(8,128)(2,1)S(1)}, bf16[128,4096]{1,0:T(8,128)(2,1)S(1)}, u32[]{:S(2)}, u32[]{:S(2)}) collective-permute-start(bf16[128,4096]{1,0:T(8,128)(2,1)S(1)} %collective-permute-done.17.mine), channel_id=1, source_target_pairs={{0,1},{1,0},{2,3},{3,2},{4,5},{5,4},{6,7},{7,6},{8,9},{9,8},{10,11... | collective-permute-start | bytes 3145736 | tf_op jit(solution)/shard_map/ppermute | solution.py:272
  113.7 19.0 %collective-permute-start.23 = (bf16[128,2048]{1,0:T(8,128)(2,1)S(1)}, bf16[128,2048]{1,0:T(8,128)(2,1)S(1)}, u32[]{:S(2)}, u32[]{:S(2)}) collective-permute-start(bf16[128,2048]{1,0:T(8,128)(2,1)S(1)} %add_convert_fusion.5), channel_id=1, source_target_pairs={{0,2},{1,3},{2,6},{3,7},{6,4},{7,5},{4,0},{5,1},{8,10},{9,11},{10,... | collective-permute-start | bytes 1572872 | tf_op jit(solution)/shard_map/ppermute | solution.py:269
  127.1 8.2 %collective-permute-start.32 = (bf16[128,2048]{1,0:T(8,128)(2,1)S(1)}, bf16[128,2048]{1,0:T(8,128)(2,1)S(1)}, u32[]{:S(2)}, u32[]{:S(2)}) collective-permute-start(bf16[128,2048]{1,0:T(8,128)(2,1)S(1)} %get-tuple-element.90), channel_id=1, source_target_pairs={{0,1},{1,0},{2,3},{3,2},{4,5},{5,4},{6,7},{7,6},{8,9},{9,8},{10,11... | collective-permute-start | bytes 1572872 | tf_op jit(solution)/shard_map/ppermute | solution.py:272
  130.4 4.8 %copy-start.3 = (bf16[1,1,128,4096]{3,2,1,0:T(8,128)(2,1)S(1)}, bf16[1,1,128,4096]{3,2,1,0:T(8,128)(2,1)}, u32[]{:S(2)}) copy-start(bf16[1,1,128,4096]{3,2,1,0:T(8,128)(2,1)} %param.8) | copy-start | bytes 3145732
  134.6 13.6 %collective-permute-start.24 = (bf16[128,2048]{1,0:T(8,128)(2,1)S(1)}, bf16[128,2048]{1,0:T(8,128)(2,1)S(1)}, u32[]{:S(2)}, u32[]{:S(2)}) collective-permute-start(bf16[128,2048]{1,0:T(8,128)(2,1)S(1)} %get-tuple-element.79), channel_id=1, source_target_pairs={{0,1},{1,0},{2,3},{3,2},{4,5},{5,4},{6,7},{7,6},{8,9},{9,8},{10,11... | collective-permute-start | bytes 1572872 | tf_op jit(solution)/shard_map/ppermute | solution.py:272
  135.2 18.9 %collective-permute-start = (bf16[128,4096]{1,0:T(8,128)(2,1)S(1)}, bf16[128,4096]{1,0:T(8,128)(2,1)S(1)}, u32[]{:S(2)}, u32[]{:S(2)}) collective-permute-start(bf16[128,4096]{1,0:T(8,128)(2,1)S(1)} %bitcast.15), channel_id=1, source_target_pairs={{0,1},{1,0},{2,3},{3,2},{4,5},{5,4},{6,7},{7,6},{8,9},{9,8},{10,11... | collective-permute-start | bytes 3145736 | tf_op jit(solution)/shard_map/ppermute | solution.py:272
  135.4 15.9 %collective-permute-start.33 = (bf16[128,2048]{1,0:T(8,128)(2,1)S(1)}, bf16[128,2048]{1,0:T(8,128)(2,1)S(1)}, u32[]{:S(2)}, u32[]{:S(2)}) collective-permute-start(bf16[128,2048]{1,0:T(8,128)(2,1)S(1)} %add_convert_fusion.2), channel_id=1, source_target_pairs={{0,2},{1,3},{2,6},{3,7},{6,4},{7,5},{4,0},{5,1},{8,10},{9,11},{10,... | collective-permute-start | bytes 1572872 | tf_op jit(solution)/shard_map/ppermute | solution.py:269
  139.8 11.5 %collective-permute-start.31 = (bf16[128,2048]{1,0:T(8,128)(2,1)S(1)}, bf16[128,2048]{1,0:T(8,128)(2,1)S(1)}, u32[]{:S(2)}, u32[]{:S(2)}) collective-permute-start(bf16[128,2048]{1,0:T(8,128)(2,1)S(1)} %get-tuple-element.87), channel_id=1, source_target_pairs={{0,1},{1,0},{2,3},{3,2},{4,5},{5,4},{6,7},{7,6},{8,9},{9,8},{10,11... | collective-permute-start | bytes 1572872 | tf_op jit(solution)/shard_map/ppermute | solution.py:272
  147.1 15.1 %collective-permute-start.19 = (bf16[128,2048]{1,0:T(8,128)(2,1)S(1)}, bf16[128,2048]{1,0:T(8,128)(2,1)S(1)}, u32[]{:S(2)}, u32[]{:S(2)}) collective-permute-start(bf16[128,2048]{1,0:T(8,128)(2,1)S(1)} %get-tuple-element.73), channel_id=1, source_target_pairs={{0,1},{1,0},{2,3},{3,2},{4,5},{5,4},{6,7},{7,6},{8,9},{9,8},{10,11... | collective-permute-start | bytes 1572872 | tf_op jit(solution)/shard_map/ppermute | solution.py:272
  148.5 15.7 %collective-permute-start.25 = (bf16[128,2048]{1,0:T(8,128)(2,1)S(1)}, bf16[128,2048]{1,0:T(8,128)(2,1)S(1)}, u32[]{:S(2)}, u32[]{:S(2)}) collective-permute-start(bf16[128,2048]{1,0:T(8,128)(2,1)S(1)} %add_convert_fusion.4), channel_id=1, source_target_pairs={{0,2},{1,3},{2,6},{3,7},{6,4},{7,5},{4,0},{5,1},{8,10},{9,11},{10,... | collective-permute-start | bytes 1572872 | tf_op jit(solution)/shard_map/ppermute | solution.py:269
  151.3 14.0 %collective-permute-start.30 = (bf16[128,2048]{1,0:T(8,128)(2,1)S(1)}, bf16[128,2048]{1,0:T(8,128)(2,1)S(1)}, u32[]{:S(2)}, u32[]{:S(2)}) collective-permute-start(bf16[128,2048]{1,0:T(8,128)(2,1)S(1)} %get-tuple-element.85), channel_id=1, source_target_pairs={{0,1},{1,0},{2,3},{3,2},{4,5},{5,4},{6,7},{7,6},{8,9},{9,8},{10,11... | collective-permute-start | bytes 1572872 | tf_op jit(solution)/shard_map/ppermute | solution.py:272
  151.5 23.9 %collective-permute-start.34 = (bf16[128,2048]{1,0:T(8,128)(2,1)S(1)}, bf16[128,2048]{1,0:T(8,128)(2,1)S(1)}, u32[]{:S(2)}, u32[]{:S(2)}) collective-permute-start(bf16[128,2048]{1,0:T(8,128)(2,1)S(1)} %add_convert_fusion.1), channel_id=1, source_target_pairs={{0,2},{1,3},{2,6},{3,7},{6,4},{7,5},{4,0},{5,1},{8,10},{9,11},{10,... | collective-permute-start | bytes 1572872 | tf_op jit(solution)/shard_map/ppermute | solution.py:269
  161.2 16.0 %collective-permute-start.14 = (bf16[128,2048]{1,0:T(8,128)(2,1)S(1)}, bf16[128,2048]{1,0:T(8,128)(2,1)S(1)}, u32[]{:S(2)}, u32[]{:S(2)}) collective-permute-start(bf16[128,2048]{1,0:T(8,128)(2,1)S(1)} %get-tuple-element.70), channel_id=1, source_target_pairs={{0,1},{1,0},{2,3},{3,2},{4,5},{5,4},{6,7},{7,6},{8,9},{9,8},{10,11... | collective-permute-start | bytes 1572872 | tf_op jit(solution)/shard_map/ppermute | solution.py:272
  162.2 15.0 %collective-permute-start.29 = (bf16[128,2048]{1,0:T(8,128)(2,1)S(1)}, bf16[128,2048]{1,0:T(8,128)(2,1)S(1)}, u32[]{:S(2)}, u32[]{:S(2)}) collective-permute-start(bf16[128,2048]{1,0:T(8,128)(2,1)S(1)} %get-tuple-element.83), channel_id=1, source_target_pairs={{0,1},{1,0},{2,3},{3,2},{4,5},{5,4},{6,7},{7,6},{8,9},{9,8},{10,11... | collective-permute-start | bytes 1572872 | tf_op jit(solution)/shard_map/ppermute | solution.py:272
  164.5 22.2 %collective-permute-start.26 = (bf16[128,2048]{1,0:T(8,128)(2,1)S(1)}, bf16[128,2048]{1,0:T(8,128)(2,1)S(1)}, u32[]{:S(2)}, u32[]{:S(2)}) collective-permute-start(bf16[128,2048]{1,0:T(8,128)(2,1)S(1)} %add_convert_fusion.3), channel_id=1, source_target_pairs={{0,2},{1,3},{2,6},{3,7},{6,4},{7,5},{4,0},{5,1},{8,10},{9,11},{10,... | collective-permute-start | bytes 1572872 | tf_op jit(solution)/shard_map/ppermute | solution.py:269
  175.7 21.4 %collective-permute-start.35 = (bf16[128,2048]{1,0:T(8,128)(2,1)S(1)}, bf16[128,2048]{1,0:T(8,128)(2,1)S(1)}, u32[]{:S(2)}, u32[]{:S(2)}) collective-permute-start(bf16[128,2048]{1,0:T(8,128)(2,1)S(1)} %add_convert_fusion), channel_id=1, source_target_pairs={{0,2},{1,3},{2,6},{3,7},{6,4},{7,5},{4,0},{5,1},{8,10},{9,11},{10,... | collective-permute-start | bytes 1572872 | tf_op jit(solution)/shard_map/ppermute | solution.py:269
Sparse Core Ops, SparseCore 0:
  19.8 45.7 all-gather.2
